TPU v7x, 256 devices: a whole 4x4x8 slice. The times are simulated.
256 devices in a mesh: island: 16 (over y, z_hi), section: 8 (over z_lo, x), tp: 2 (over core).
Axes of the slice: x: 4, y: 4, z: 8 (z_hi: 4, z_lo: 2; z = z_hi * 2 + z_lo), core: 2. Of those that a mesh axis runs over, the one named last changes fastest.
Arguments:
- tokens: bfloat16 [3072, 3584], P('island', 'tp'), may hold values from -6 to 6
- cotangent: bfloat16 [3072, 3584], P('island', 'tp'), may hold values from -6 to 6
- master: float32 [8, 3584, 3584], P('section', 'island', 'tp'), may hold values from -0.09375 to 0.09375
Outputs:
- in_grads: bfloat16 [8, 3072, 3584], P('section', 'island', 'tp')
- new_master: float32 [8, 3584, 3584], P('section', 'island', 'tp')
All inputs are finite; a program needn't handle non-finite values.
Results may differ from a plain program's by a relative error of at most 0.025.
Values may be sent and summed in bfloat16 or wider, within the bound.
No kernel may reach another device: no remote copies, remote signals or barrier semaphores. Data moves between devices by JAX's collectives and lax.ppermute only.
A program may use at most 64 MiB of HBM per device.

v0:
```python
import functools

import jax
import jax.numpy as jnp
from jax import lax
from jax.experimental import pallas as pl
from jax.experimental.pallas import tpu as pltpu
from jax.sharding import PartitionSpec as P

D = 3584
HALF = 1792
MICRO = 4
MB = 48
SECTIONS = 8
ISLANDS = 16
SIDE = 4
ROWS = D // ISLANDS
FORWARD_TICKS = MICRO + SECTIONS - 1
TICKS = FORWARD_TICKS + SECTIONS
SPLIT = 1024
ROW_CHUNKS = (96, 128)
EARLY = 2
NORM_EPS = 1e-05
STEP_SIZE = 1.0
F32 = jnp.float32
BF16 = jnp.bfloat16
N_TILE = 256
K_TILE = 256
LIMIT_MB = 8
PARAMS = pltpu.CompilerParams(vmem_limit_bytes=LIMIT_MB * 1024 * 1024)
VMEM = pl.BlockSpec(memory_space=pltpu.VMEM)
SMEM = pl.BlockSpec(memory_space=pltpu.SMEM)


def half_rows(half, start, size):
    return pl.ds(pl.multiple_of(half * HALF + start, 256), size)


def slot_of(micro):
    return jnp.where((micro >= 0) & (micro < MICRO), micro, MICRO)


def backward_micro(tick, section):
    return tick - (2 * SECTIONS - 1) + section


def forward_kernel(
    tick, first, ids, own, other, next_tokens, weights_a, weights_b, *refs
):
    send, x_slots, preacts, scales = refs if first else refs[3:]
    tp_id = ids[0]
    is_last = ids[1] == SECTIONS - 1
    slot = slot_of(tick - ids[1])
    x_slots[slot, tp_id] = own[...]
    x_slots[slot, 1 - tp_id] = other[...]
    own_float = own[...].astype(F32)
    other_float = other[...].astype(F32)
    square_sum = jnp.sum(own_float * own_float, axis=1, keepdims=True)
    square_sum += jnp.sum(other_float * other_float, axis=1, keepdims=True)
    row_scale = lax.rsqrt(square_sum / D + NORM_EPS)
    scales[slot] = jnp.broadcast_to(row_scale, scales.shape[1:])
    for start in range(0, HALF, N_TILE):
        cols = pl.ds(start, N_TILE)
        weights = weights_a if start < SPLIT else weights_b
        part = pl.ds(start if start < SPLIT else start - SPLIT, N_TILE)
        product = jnp.dot(
            own[...], weights[half_rows(tp_id, 0, HALF), part], preferred_element_type=F32
        )
        product += jnp.dot(
            other[...], weights[half_rows(1 - tp_id, 0, HALF), part], preferred_element_type=F32
        )
        value = product * row_scale
        preacts[slot, :, cols] = value
        output = own[:, cols].astype(F32) + value / (1.0 + jnp.exp(-value))
        output = output.astype(BF16).astype(F32)
        send[:, cols] = jnp.where(is_last, next_tokens[:, cols].astype(F32), output).astype(BF16)


STASH = (
    jax.ShapeDtypeStruct((MICRO + 1, 2, MB, HALF), BF16),
    jax.ShapeDtypeStruct((MICRO + 1, MB, HALF), F32),
    jax.ShapeDtypeStruct((MICRO + 1, MB, 128), F32),
)


def forward_tick(tick, ids, own, other, next_tokens, weights, stash):
    first = not stash
    return pl.pallas_call(
        functools.partial(forward_kernel, tick, first),
        out_shape=(jax.ShapeDtypeStruct(own.shape, BF16), *STASH),
        in_specs=[SMEM] + [VMEM] * (5 + len(stash)),
        out_specs=(VMEM,) * 4,
        input_output_aliases={} if first else {6: 1, 7: 2, 8: 3},
        compiler_params=PARAMS,
        cost_estimate=pl.CostEstimate(
            flops=2 * MB * D * HALF, bytes_accessed=2 * D * HALF, transcendentals=MB * HALF
        ),
        name="forward_tick",
    )(ids, own, other, next_tokens, *weights, *stash)


def backward_kernel(
    tick, first, ids, grad, x_slots, preacts, scales, weights_a, weights_b, *refs
):
    own_part, other_part, deltas, scaled = refs if first else refs[1:]
    tp_id = ids[0]
    slot = slot_of(backward_micro(tick, ids[1]))
    row_scale = scales[slot, :, :1]
    mean_prod = jnp.zeros((MB, 1), F32)
    for start in range(0, HALF, N_TILE):
        cols = pl.ds(start, N_TILE)
        value = preacts[slot, :, cols]
        sig_value = 1.0 / (1.0 + jnp.exp(-value))
        delta = grad[:, cols].astype(F32) * (sig_value * (1.0 + value * (1.0 - sig_value)))
        mean_prod += jnp.sum(delta * value, axis=1, keepdims=True)
        scaled[:, cols] = (delta * row_scale).astype(BF16)
    shift = row_scale * row_scale * (mean_prod / D)
    deltas[slot] = scaled[...]
    across = (((1,), (1,)), ((), ()))
    for start in range(0, HALF, K_TILE):
        cols = pl.ds(start, K_TILE)
        for half, out in ((1 - tp_id, other_part), (tp_id, own_part)):
            rows = half_rows(half, start, K_TILE)
            product = lax.dot_general(
                scaled[:, :SPLIT], weights_a[rows, :], across, preferred_element_type=F32
            )
            product += lax.dot_general(
                scaled[:, SPLIT:], weights_b[rows, :], across, preferred_element_type=F32
            )
            product -= x_slots[slot, half, :, cols].astype(F32) * shift
            out[:, cols] = product.astype(out.dtype)


def backward_tick(tick, ids, grad, stash, weights, deltas):
    first = not deltas
    return pl.pallas_call(
        functools.partial(backward_kernel, tick, first),
        out_shape=(
            jax.ShapeDtypeStruct((MB, HALF), F32),
            jax.ShapeDtypeStruct((MB, HALF), BF16),
            jax.ShapeDtypeStruct((MICRO + 1, MB, HALF), BF16),
        ),
        in_specs=[SMEM] + [VMEM] * (6 + len(deltas)),
        out_specs=(VMEM,) * 3,
        scratch_shapes=[pltpu.VMEM((MB, HALF), BF16)],
        input_output_aliases={} if first else {7: 2},
        compiler_params=PARAMS,
        cost_estimate=pl.CostEstimate(
            flops=2 * MB * D * HALF, bytes_accessed=2 * D * HALF, transcendentals=MB * HALF
        ),
        name="backward_tick",
    )(ids, grad, *stash, *weights, *deltas)


def swap_cores(value):
    return lax.ppermute(value, "tp", [(0, 1), (1, 0)])


def to_section(value, step):
    return lax.ppermute(value, "section", [(s, (s + step) % SECTIONS) for s in range(SECTIONS)])


def along_y(value, step):
    pairs = [(i, (i // SIDE + step) % SIDE * SIDE + i % SIDE) for i in range(ISLANDS)]
    return lax.ppermute(value, "island", pairs)


def along_z(value, step):
    pairs = [(i, i // SIDE * SIDE + (i % SIDE + step) % SIDE) for i in range(ISLANDS)]
    return lax.ppermute(value, "island", pairs)


def ring_gather(block, shift, place, target, at):
    half = block.shape[0] // 2
    below, above = shift(block, 1), shift(block, -1)
    far_low, far_high = shift(below[:half], 1), shift(above[half:], -1)
    target = at(target, place, block, 0)
    target = at(target, (place + SIDE - 1) % SIDE, below, 0)
    target = at(target, (place + 1) % SIDE, above, 0)
    target = at(target, (place + 2) % SIDE, far_low, 0)
    return at(target, (place + 2) % SIDE, far_high, half)


def gather_islands(block, target, row_start):
    island = lax.axis_index("island")
    y_place, z_place = island // SIDE, island % SIDE
    tail = (1,) * (target.ndim - 4)

    def at_z(buffer, position, piece, start):
        return lax.dynamic_update_slice(buffer, piece[None], (position, start, 0))

    def at_y(buffer, position, piece, start):
        piece = piece.reshape(1, *piece.shape[:1], *tail, *piece.shape[1:])
        return lax.dynamic_update_slice(
            buffer, piece, (position, start, row_start) + (0,) * (buffer.ndim - 3)
        )

    column = ring_gather(block, along_z, z_place, jnp.zeros((SIDE, *block.shape), BF16), at_z)
    return ring_gather(column, along_y, y_place, target, at_y), column


def after(value, earlier):
    return lax.optimization_barrier((value, earlier))[0]


def gather_weights(rows):
    by_gather = lax.all_gather(rows[:, :SPLIT], "island", axis=0, tiled=True)
    by_rings = jnp.zeros((SIDE, SIDE, ROWS, HALF - SPLIT), BF16)
    start = 0
    for size in ROW_CHUNKS:
        block = rows[start : start + size, SPLIT:]
        by_rings, _ = gather_islands(block, by_rings, start)
        start += size
    return by_gather, by_rings.reshape(D, HALF - SPLIT)


def exchange_x(x_slots, tp_id, earlier):
    count = MICRO // 2
    part = lax.dynamic_slice_in_dim(x_slots, tp_id * count, count, 0)
    part = part.reshape(count, 2, MB, ISLANDS // 2, ROWS).transpose(1, 3, 0, 2, 4)
    part = after(part.reshape(ISLANDS, count * MB, ROWS), earlier)
    return lax.all_to_all(part, "island", 0, 0)


def body(tokens, cotangent, master):
    island_count = lax.axis_size("island")
    section_id = lax.axis_index("section")
    tp_id = lax.axis_index("tp")
    ids = jnp.stack([tp_id, section_id]).astype(jnp.int32)
    tok_blocks = [tokens[m * MB : (m + 1) * MB] for m in range(MICRO)]
    cot_blocks = [cotangent[m * MB : (m + 1) * MB] for m in range(MICRO)]
    weights = gather_weights(master[0].astype(BF16))

    tok_blocks, cot_blocks = lax.optimization_barrier((tok_blocks, cot_blocks))
    stash, deltas = (), None
    grads = jnp.zeros((MICRO + 1, MB, HALF), BF16)
    own, grad = tok_blocks[0], cot_blocks[0]
    for tick in range(TICKS):
        if tick < FORWARD_TICKS:
            other = swap_cores(own)
            following = tok_blocks[min(tick + 1, MICRO - 1)]
            send, *stash = forward_tick(tick, ids, own, other, following, weights, stash)
            if tick < FORWARD_TICKS - 1:
                own = to_section(send, 1)
        if tick >= SECTIONS:
            own_part, other_part, deltas = backward_tick(
                tick, ids, grad, stash, weights, () if deltas is None else (deltas,)
            )
            received = swap_cores(other_part)
            grad_out = (grad.astype(F32) + own_part + received.astype(F32)).astype(BF16)
            slot = slot_of(backward_micro(tick, section_id))
            grads = lax.dynamic_update_slice_in_dim(grads, grad_out[None], slot, 0)
            if tick < TICKS - 1:
                following = cot_blocks[min(tick + 1 - SECTIONS, MICRO - 1)]
                passed = jnp.where(section_id == 0, following, grad_out)
                grad = to_section(passed, -1)
        micro = tick - (2 * SECTIONS - 1)
        if micro == EARLY - 1:
            early_deltas = lax.all_gather(deltas[:EARLY], "island")

    x_slots, deltas, empty = lax.optimization_barrier((stash[0], deltas, jnp.zeros((), BF16)))
    ring_deltas = jnp.broadcast_to(empty, (SIDE, SIDE, MICRO - EARLY, MB, HALF))
    block = deltas[EARLY]
    for micro in range(EARLY, MICRO):
        ring_deltas, column = gather_islands(block, ring_deltas, micro - EARLY)
        if micro < MICRO - 1:
            block = after(deltas[micro + 1], column)
    x_part = exchange_x(x_slots, tp_id, column)

    x_other = swap_cores(x_part)

    def outer(x_rows, delta_rows):
        return lax.dot_general(
            x_rows.reshape(-1, ROWS),
            delta_rows.reshape(-1, HALF),
            (((0,), (0,)), ((), ())),
            preferred_element_type=F32,
        )

    late_rows = outer(jnp.where(tp_id == 1, x_part, x_other), ring_deltas)
    late_rows = lax.optimization_barrier(late_rows)
    grad_rows = late_rows + outer(jnp.where(tp_id == 0, x_part, x_other), early_deltas)
    updated = master[0] - STEP_SIZE * grad_rows / (MICRO * MB * island_count)
    return (grads[:MICRO].reshape(1, MICRO * MB, HALF), updated[None])


def solution(mesh):
    placed = (P("island", "tp"), P("island", "tp"), P("section", "island", "tp"))
    return jax.shard_map(
        body,
        mesh=mesh,
        in_specs=placed,
        out_specs=(P("section", "island", "tp"), P("section", "island", "tp")),
        check_vma=False,
    )
```

profile of v0, /device:TPU:56, one launch (start us, length us, event | category | flops | bytes accessed | tf_op | source)
XLA Modules:
  0.0 578.5 jit_solution(13230056224639556324)
XLA Ops:
  9.6 3.3 collective-permute-start.1
  22.2 3.9 collective-permute-done.1
  26.1 4.2 collective-permute-start.4
  30.3 5.9 %collective-permute-done.9 = bf16[128,768]{1,0:T(8,128)(2,1)S(1)} collective-permute-done((bf16[128,768]{1,0:T(8,128)(2,1)S(1)}, bf16[128,768]{1,0:T(8,128)(2,1)S(1)}, u32[]{:S(2)}, u32[]{:S(2)}) %collective-permute-start.9) | collective-permute-done | bytes 196640 | tf_op jit(solution)/shard_map/ppermute | solution.py:170
  36.7 3.8 collective-permute-start.12
  52.2 10.7 %collective-permute-done.5 = bf16[4,96,768]{2,1,0:T(8,128)(2,1)} collective-permute-done((bf16[4,96,768]{2,1,0:T(8,128)(2,1)S(1)}, bf16[4,96,768]{2,1,0:T(8,128)(2,1)}, u32[]{:S(2)}, u32[]{:S(2)}) %collective-permute-start.5) | collective-permute-done | bytes 589856 | tf_op jit(solution)/shard_map/ppermute | solution.py:165
  69.5 23.0 %collective-permute-done.13 = bf16[4,128,768]{2,1,0:T(8,128)(2,1)S(1)} collective-permute-done((bf16[4,128,768]{2,1,0:T(8,128)(2,1)S(1)}, bf16[4,128,768]{2,1,0:T(8,128)(2,1)S(1)}, u32[]{:S(2)}, u32[]{:S(2)}) %collective-permute-start.13) | collective-permute-done | bytes 786464 | tf_op jit(solution)/shard_map/ppermute | solution.py:165
  95.9 8.7 %collective-permute-done.7 = bf16[2,96,768]{2,1,0:T(8,128)(2,1)S(1)} collective-permute-done((bf16[2,96,768]{2,1,0:T(8,128)(2,1)S(1)}, bf16[2,96,768]{2,1,0:T(8,128)(2,1)S(1)}, u32[]{:S(2)}, u32[]{:S(2)}) %collective-permute-start.7) | collective-permute-done | bytes 294944 | tf_op jit(solution)/shard_map/ppermute | solution.py:165
  106.8 6.5 %collective-permute-done.15 = bf16[2,128,768]{2,1,0:T(8,128)(2,1)S(1)} collective-permute-done((bf16[2,128,768]{2,1,0:T(8,128)(2,1)S(1)}, bf16[2,128,768]{2,1,0:T(8,128)(2,1)S(1)}, u32[]{:S(2)}, u32[]{:S(2)}) %collective-permute-start.15) | collective-permute-done | bytes 393248 | tf_op jit(solution)/shard_map/ppermute | solution.py:165
  118.3 10.7 %all-gather.4.cloned.1.call-done.weights_a = bf16[3584,1024]{1,0:T(8,128)(2,1)} async-done(((bf16[224,1024]{1,0:T(8,128)(2,1)}), bf16[3584,1024]{1,0:T(8,128)(2,1)}) %all-gather.4.cloned.1.call-update) | async-done | bytes 7340048 | tf_op jit(solution)/shard_map/all_gather | solution.py:207
  129.0 3.1 copy-done
  142.5 6.5 %collective-permute-done.17.own = bf16[48,1792]{1,0:T(8,128)(2,1)S(1)} collective-permute-done((bf16[48,1792]{1,0:T(8,128)(2,1)S(1)}, bf16[48,1792]{1,0:T(8,128)(2,1)S(1)}, u32[]{:S(2)}, u32[]{:S(2)}) %collective-permute-start.17) | collective-permute-done | bytes 172064 | tf_op jit(solution)/shard_map/ppermute | solution.py:160
  153.5 8.5 %collective-permute-done.19.own = bf16[48,1792]{1,0:T(8,128)(2,1)S(1)} collective-permute-done((bf16[48,1792]{1,0:T(8,128)(2,1)S(1)}, bf16[48,1792]{1,0:T(8,128)(2,1)S(1)}, u32[]{:S(2)}, u32[]{:S(2)}) %collective-permute-start.19) | collective-permute-done | bytes 172064 | tf_op jit(solution)/shard_map/ppermute | solution.py:160
  166.5 8.5 %collective-permute-done.21.own = bf16[48,1792]{1,0:T(8,128)(2,1)S(1)} collective-permute-done((bf16[48,1792]{1,0:T(8,128)(2,1)S(1)}, bf16[48,1792]{1,0:T(8,128)(2,1)S(1)}, u32[]{:S(2)}, u32[]{:S(2)}) %collective-permute-start.21) | collective-permute-done | bytes 172064 | tf_op jit(solution)/shard_map/ppermute | solution.py:160
  179.7 8.5 %collective-permute-done.23.own = bf16[48,1792]{1,0:T(8,128)(2,1)S(1)} collective-permute-done((bf16[48,1792]{1,0:T(8,128)(2,1)S(1)}, bf16[48,1792]{1,0:T(8,128)(2,1)S(1)}, u32[]{:S(2)}, u32[]{:S(2)}) %collective-permute-start.23) | collective-permute-done | bytes 172064 | tf_op jit(solution)/shard_map/ppermute | solution.py:160
  192.8 8.5 %collective-permute-done.25.own = bf16[48,1792]{1,0:T(8,128)(2,1)S(1)} collective-permute-done((bf16[48,1792]{1,0:T(8,128)(2,1)S(1)}, bf16[48,1792]{1,0:T(8,128)(2,1)S(1)}, u32[]{:S(2)}, u32[]{:S(2)}) %collective-permute-start.25) | collective-permute-done | bytes 172064 | tf_op jit(solution)/shard_map/ppermute | solution.py:160
  205.8 8.5 %collective-permute-done.27.own = bf16[48,1792]{1,0:T(8,128)(2,1)S(1)} collective-permute-done((bf16[48,1792]{1,0:T(8,128)(2,1)S(1)}, bf16[48,1792]{1,0:T(8,128)(2,1)S(1)}, u32[]{:S(2)}, u32[]{:S(2)}) %collective-permute-start.27) | collective-permute-done | bytes 172064 | tf_op jit(solution)/shard_map/ppermute | solution.py:160
  218.8 8.5 %collective-permute-done.29.own = bf16[48,1792]{1,0:T(8,128)(2,1)S(1)} collective-permute-done((bf16[48,1792]{1,0:T(8,128)(2,1)S(1)}, bf16[48,1792]{1,0:T(8,128)(2,1)S(1)}, u32[]{:S(2)}, u32[]{:S(2)}) %collective-permute-start.29) | collective-permute-done | bytes 172064 | tf_op jit(solution)/shard_map/ppermute | solution.py:160
  232.2 8.5 %collective-permute-done.31.own = bf16[48,1792]{1,0:T(8,128)(2,1)S(1)} collective-permute-done((bf16[48,1792]{1,0:T(8,128)(2,1)S(1)}, bf16[48,1792]{1,0:T(8,128)(2,1)S(1)}, u32[]{:S(2)}, u32[]{:S(2)}) %collective-permute-start.31) | collective-permute-done | bytes 172064 | tf_op jit(solution)/shard_map/ppermute | solution.py:160
  242.1 3.7 forward_tick.19
  245.8 5.3 backward_tick.11
  256.6 3.9 collective-permute-start.34
  260.5 3.1 copy-done.2
  268.0 3.5 forward_tick.20
  271.8 4.6 backward_tick.12
  276.5 3.5 collective-permute-done.39.own
  282.8 3.7 forward_tick.21
  287.5 4.6 backward_tick.13
  294.4 3.9 collective-permute-start.42
  298.3 3.9 collective-permute-done.42.grad
  302.3 4.6 backward_tick.14
  309.2 4.6 collective-permute-start.44
  313.8 3.9 collective-permute-done.44.grad
  321.5 4.6 backward_tick.15
  329.3 4.6 collective-permute-start.46
  333.9 4.3 collective-permute-done.46.grad
  338.1 3.1 copy-done.3
  347.9 4.6 backward_tick.16
  354.3 5.0 collective-permute-start.48
  360.0 3.6 collective-permute-done.48.grad
  363.6 4.6 backward_tick.17
  369.8 4.7 collective-permute-start.50
  375.2 3.3 collective-permute-done.50.grad
  378.4 4.6 backward_tick.18
  384.6 4.7 collective-permute-start.52
  390.0 3.3 collective-permute-done.52.grad
  393.2 4.6 backward_tick.19
  399.4 4.8 collective-permute-start.54
  408.2 3.1 copy-done.4
  418.1 4.6 backward_tick.20
  424.3 4.8 collective-permute-start.56
  429.7 5.1 collective-permute-done.56.grad
  434.8 3.1 copy-done.5
  437.9 4.6 backward_tick.21
  449.7 21.2 %collective-permute-done.58 = bf16[48,1792]{1,0:T(8,128)(2,1)S(1)} collective-permute-done((bf16[48,1792]{1,0:T(8,128)(2,1)S(1)}, bf16[48,1792]{1,0:T(8,128)(2,1)S(1)}, u32[]{:S(2)}, u32[]{:S(2)}) %collective-permute-start.58) | collective-permute-done | bytes 172064 | tf_op jit(solution)/shard_map/ppermute | solution.py:170
  478.0 5.7 collective-permute-done.60
  483.7 13.0 %collective-permute-done.61 = bf16[24,1792]{1,0:T(8,128)(2,1)S(1)} collective-permute-done((bf16[24,1792]{1,0:T(8,128)(2,1)S(1)}, bf16[24,1792]{1,0:T(8,128)(2,1)S(1)}, u32[]{:S(2)}, u32[]{:S(2)}) %collective-permute-start.61) | collective-permute-done | bytes 86048 | tf_op jit(solution)/shard_map/ppermute | solution.py:170
  497.6 3.6 collective-permute-start.63
  511.1 4.2 collective-permute-start.65
  519.8 9.2 %all-to-all-start = ((bf16[16,96,224]{2,1,0:T(8,128)(2,1)}), bf16[16,96,224]{2,1,0:T(8,128)(2,1)S(1)}, u32[]{:S(2)}, u32[]{:S(2)}) async-start(bf16[16,96,224]{2,1,0:T(8,128)(2,1)} %bitcast.37), calls=%async_computation | async-start | bytes 1572864 | tf_op jit(solution)/shard_map/all_to_all | solution.py:222
  535.1 6.8 %collective-permute-done.71 = bf16[4,48,1792]{2,1,0:T(8,128)(2,1)} collective-permute-done((bf16[4,48,1792]{2,1,0:T(8,128)(2,1)S(1)}, bf16[4,48,1792]{2,1,0:T(8,128)(2,1)}, u32[]{:S(2)}, u32[]{:S(2)}) %collective-permute-start.71) | collective-permute-done | bytes 688160 | tf_op jit(solution)/shard_map/ppermute | solution.py:165
  547.5 4.4 collective-permute-done.69
  561.6 4.0 fusion.5
  565.6 4.1 fusion.6
  (327 shorter events, 190.6 us)
Async XLA Ops:
  7.2 121.8 %all-gather.4.cloned.1.call-start = ((), (), s32[]{:S(2)}) async-start(), calls=%async_computation.1 | async-start | bytes 7798784 | tf_op jit(solution)/shard_map/all_gather | solution.py:207
  9.6 556.0 %all-gather.6.cloned.1.call-start = ((), (), s32[]{:S(2)}) async-start(), calls=%async_computation.2 | async-start | bytes 5849088 | tf_op jit(solution)/shard_map/all_gather | solution.py:259
  9.6 16.4 %collective-permute-start.1 = (bf16[96,768]{1,0:T(8,128)(2,1)S(1)}, bf16[96,768]{1,0:T(8,128)(2,1)S(1)}, u32[]{:S(2)}, u32[]{:S(2)}) collective-permute-start(bf16[96,768]{1,0:T(8,128)(2,1)S(1)} %slice.125), channel_id=1, source_target_pairs={{0,16},{16,32},{32,48},{48,0},{64,80},{80,96},{96,112},{112,64},{1... | collective-permute-start | bytes 442376 | tf_op jit(solution)/shard_map/ppermute | solution.py:170
  13.0 13.1 %collective-permute-start.2 = (bf16[96,768]{1,0:T(8,128)(2,1)S(1)}, bf16[96,768]{1,0:T(8,128)(2,1)S(1)}, u32[]{:S(2)}, u32[]{:S(2)}) collective-permute-start(bf16[96,768]{1,0:T(8,128)(2,1)S(1)} %slice.125), channel_id=1, source_target_pairs={{0,48},{16,0},{32,16},{48,32},{64,112},{80,64},{96,80},{112,96},{1... | collective-permute-start | bytes 442376 | tf_op jit(solution)/shard_map/ppermute | solution.py:170
  15.2 21.0 %collective-permute-start.9 = (bf16[128,768]{1,0:T(8,128)(2,1)S(1)}, bf16[128,768]{1,0:T(8,128)(2,1)S(1)}, u32[]{:S(2)}, u32[]{:S(2)}) collective-permute-start(bf16[128,768]{1,0:T(8,128)(2,1)S(1)} %slice.130), channel_id=1, source_target_pairs={{0,16},{16,32},{32,48},{48,0},{64,80},{80,96},{96,112},{112,64},{1... | collective-permute-start | bytes 589832 | tf_op jit(solution)/shard_map/ppermute | solution.py:170
  16.7 20.0 %collective-permute-start.10 = (bf16[128,768]{1,0:T(8,128)(2,1)S(1)}, bf16[128,768]{1,0:T(8,128)(2,1)S(1)}, u32[]{:S(2)}, u32[]{:S(2)}) collective-permute-start(bf16[128,768]{1,0:T(8,128)(2,1)S(1)} %slice.130), channel_id=1, source_target_pairs={{0,48},{16,0},{32,16},{48,32},{64,112},{80,64},{96,80},{112,96},{1... | collective-permute-start | bytes 589832 | tf_op jit(solution)/shard_map/ppermute | solution.py:170
  21.9 95.7 %collective-permute-start = (bf16[48,1792]{1,0:T(8,128)(2,1)S(1)}, bf16[48,1792]{1,0:T(8,128)(2,1)S(1)}, u32[]{:S(2)}, u32[]{:S(2)}) collective-permute-start(bf16[48,1792]{1,0:T(8,128)(2,1)S(1)} %get-tuple-element.92.own), channel_id=1, source_target_pairs={{0,1},{1,0},{2,3},{3,2},{4,5},{5,4},{6,7},{7,6},{8,9},{9,8},{10,11... | collective-permute-start | bytes 516104 | tf_op jit(solution)/shard_map/ppermute | solution.py:156
  26.0 15.8 %collective-permute-start.3 = (bf16[48,768]{1,0:T(8,128)(2,1)S(1)}, bf16[48,768]{1,0:T(8,128)(2,1)S(1)}, u32[]{:S(2)}, u32[]{:S(2)}) collective-permute-start(bf16[48,768]{1,0:T(8,128)(2,1)S(1)} %slice.126), channel_id=1, source_target_pairs={{0,16},{16,32},{32,48},{48,0},{64,80},{80,96},{96,112},{112,64},{1... | collective-permute-start | bytes 221192 | tf_op jit(solution)/shard_map/ppermute | solution.py:170
  26.1 18.1 %collective-permute-start.4 = (bf16[48,768]{1,0:T(8,128)(2,1)S(1)}, bf16[48,768]{1,0:T(8,128)(2,1)S(1)}, u32[]{:S(2)}, u32[]{:S(2)}) collective-permute-start(bf16[48,768]{1,0:T(8,128)(2,1)S(1)} %slice.127), channel_id=1, source_target_pairs={{0,48},{16,0},{32,16},{48,32},{64,112},{80,64},{96,80},{112,96},{1... | collective-permute-start | bytes 221192 | tf_op jit(solution)/shard_map/ppermute | solution.py:170
  36.2 10.5 %collective-permute-start.11 = (bf16[64,768]{1,0:T(8,128)(2,1)S(1)}, bf16[64,768]{1,0:T(8,128)(2,1)S(1)}, u32[]{:S(2)}, u32[]{:S(2)}) collective-permute-start(bf16[64,768]{1,0:T(8,128)(2,1)S(1)} %slice.131), channel_id=1, source_target_pairs={{0,16},{16,32},{32,48},{48,0},{64,80},{80,96},{96,112},{112,64},{1... | collective-permute-start | bytes 294920 | tf_op jit(solution)/shard_map/ppermute | solution.py:170
  36.7 12.7 %collective-permute-start.12 = (bf16[64,768]{1,0:T(8,128)(2,1)S(1)}, bf16[64,768]{1,0:T(8,128)(2,1)S(1)}, u32[]{:S(2)}, u32[]{:S(2)}) collective-permute-start(bf16[64,768]{1,0:T(8,128)(2,1)S(1)} %slice.132), channel_id=1, source_target_pairs={{0,48},{16,0},{32,16},{48,32},{64,112},{80,64},{96,80},{112,96},{1... | collective-permute-start | bytes 294920 | tf_op jit(solution)/shard_map/ppermute | solution.py:170
  44.2 18.7 %collective-permute-start.5 = (bf16[4,96,768]{2,1,0:T(8,128)(2,1)S(1)}, bf16[4,96,768]{2,1,0:T(8,128)(2,1)}, u32[]{:S(2)}, u32[]{:S(2)}) collective-permute-start(bf16[4,96,768]{2,1,0:T(8,128)(2,1)S(1)} %bitcast_dynamic-update-slice_fusion.47), channel_id=1, source_target_pairs={{0,64},{16,80},{32,96},{48,112},{64,128},{80,144},{96,160},{112,17... | collective-permute-start | bytes 1769480 | tf_op jit(solution)/shard_map/ppermute | solution.py:165
  44.3 21.7 %collective-permute-start.6 = (bf16[4,96,768]{2,1,0:T(8,128)(2,1)S(1)}, bf16[4,96,768]{2,1,0:T(8,128)(2,1)}, u32[]{:S(2)}, u32[]{:S(2)}) collective-permute-start(bf16[4,96,768]{2,1,0:T(8,128)(2,1)S(1)} %bitcast_dynamic-update-slice_fusion.47), channel_id=1, source_target_pairs={{0,192},{16,208},{32,224},{48,240},{64,0},{80,16},{96,32},{112,48}... | collective-permute-start | bytes 1769480 | tf_op jit(solution)/shard_map/ppermute | solution.py:165
  49.4 43.1 %collective-permute-start.13 = (bf16[4,128,768]{2,1,0:T(8,128)(2,1)S(1)}, bf16[4,128,768]{2,1,0:T(8,128)(2,1)S(1)}, u32[]{:S(2)}, u32[]{:S(2)}) collective-permute-start(bf16[4,128,768]{2,1,0:T(8,128)(2,1)S(1)} %bitcast_dynamic-update-slice_fusion.41), channel_id=1, source_target_pairs={{0,64},{16,80},{32,96},{48,112},{64,128},{80,144},{96,160},{112,17... | collective-permute-start | bytes 2359304 | tf_op jit(solution)/shard_map/ppermute | solution.py:165
  49.5 45.1 %collective-permute-start.14 = (bf16[4,128,768]{2,1,0:T(8,128)(2,1)S(1)}, bf16[4,128,768]{2,1,0:T(8,128)(2,1)S(1)}, u32[]{:S(2)}, u32[]{:S(2)}) collective-permute-start(bf16[4,128,768]{2,1,0:T(8,128)(2,1)S(1)} %bitcast_dynamic-update-slice_fusion.41), channel_id=1, source_target_pairs={{0,192},{16,208},{32,224},{48,240},{64,0},{80,16},{96,32},{112,48}... | collective-permute-start | bytes 2359304 | tf_op jit(solution)/shard_map/ppermute | solution.py:165
  63.8 40.8 %collective-permute-start.7 = (bf16[2,96,768]{2,1,0:T(8,128)(2,1)S(1)}, bf16[2,96,768]{2,1,0:T(8,128)(2,1)S(1)}, u32[]{:S(2)}, u32[]{:S(2)}) collective-permute-start(bf16[2,96,768]{2,1,0:T(8,128)(2,1)S(1)} %slice.128), channel_id=1, source_target_pairs={{0,64},{16,80},{32,96},{48,112},{64,128},{80,144},{96,160},{112,17... | collective-permute-start | bytes 884744 | tf_op jit(solution)/shard_map/ppermute | solution.py:165
  67.0 39.6 %collective-permute-start.8 = (bf16[2,96,768]{2,1,0:T(8,128)(2,1)S(1)}, bf16[2,96,768]{2,1,0:T(8,128)(2,1)S(1)}, u32[]{:S(2)}, u32[]{:S(2)}) collective-permute-start(bf16[2,96,768]{2,1,0:T(8,128)(2,1)S(1)} %slice.129), channel_id=1, source_target_pairs={{0,192},{16,208},{32,224},{48,240},{64,0},{80,16},{96,32},{112,48}... | collective-permute-start | bytes 884744 | tf_op jit(solution)/shard_map/ppermute | solution.py:165
  92.5 20.8 %collective-permute-start.15 = (bf16[2,128,768]{2,1,0:T(8,128)(2,1)S(1)}, bf16[2,128,768]{2,1,0:T(8,128)(2,1)S(1)}, u32[]{:S(2)}, u32[]{:S(2)}) collective-permute-start(bf16[2,128,768]{2,1,0:T(8,128)(2,1)S(1)} %slice.133), channel_id=1, source_target_pairs={{0,64},{16,80},{32,96},{48,112},{64,128},{80,144},{96,160},{112,17... | collective-permute-start | bytes 1179656 | tf_op jit(solution)/shard_map/ppermute | solution.py:165
  94.7 20.5 %collective-permute-start.16 = (bf16[2,128,768]{2,1,0:T(8,128)(2,1)S(1)}, bf16[2,128,768]{2,1,0:T(8,128)(2,1)S(1)}, u32[]{:S(2)}, u32[]{:S(2)}) collective-permute-start(bf16[2,128,768]{2,1,0:T(8,128)(2,1)S(1)} %slice.134), channel_id=1, source_target_pairs={{0,192},{16,208},{32,224},{48,240},{64,0},{80,16},{96,32},{112,48}... | collective-permute-start | bytes 1179656 | tf_op jit(solution)/shard_map/ppermute | solution.py:165
  140.4 8.5 %collective-permute-start.17 = (bf16[48,1792]{1,0:T(8,128)(2,1)S(1)}, bf16[48,1792]{1,0:T(8,128)(2,1)S(1)}, u32[]{:S(2)}, u32[]{:S(2)}) collective-permute-start(bf16[48,1792]{1,0:T(8,128)(2,1)S(1)} %get-tuple-element.94), channel_id=1, source_target_pairs={{0,2},{2,4},{4,6},{6,8},{8,10},{10,12},{12,14},{14,0},{1,3},{3,5},... | collective-permute-start | bytes 516104 | tf_op jit(solution)/shard_map/ppermute | solution.py:160
  153.4 8.6 %collective-permute-start.19 = (bf16[48,1792]{1,0:T(8,128)(2,1)S(1)}, bf16[48,1792]{1,0:T(8,128)(2,1)S(1)}, u32[]{:S(2)}, u32[]{:S(2)}) collective-permute-start(bf16[48,1792]{1,0:T(8,128)(2,1)S(1)} %get-tuple-element.99), channel_id=1, source_target_pairs={{0,2},{2,4},{4,6},{6,8},{8,10},{10,12},{12,14},{14,0},{1,3},{3,5},... | collective-permute-start | bytes 516104 | tf_op jit(solution)/shard_map/ppermute | solution.py:160
  166.4 8.6 %collective-permute-start.21 = (bf16[48,1792]{1,0:T(8,128)(2,1)S(1)}, bf16[48,1792]{1,0:T(8,128)(2,1)S(1)}, u32[]{:S(2)}, u32[]{:S(2)}) collective-permute-start(bf16[48,1792]{1,0:T(8,128)(2,1)S(1)} %get-tuple-element.104), channel_id=1, source_target_pairs={{0,2},{2,4},{4,6},{6,8},{8,10},{10,12},{12,14},{14,0},{1,3},{3,5},... | collective-permute-start | bytes 516104 | tf_op jit(solution)/shard_map/ppermute | solution.py:160
  179.6 8.6 %collective-permute-start.23 = (bf16[48,1792]{1,0:T(8,128)(2,1)S(1)}, bf16[48,1792]{1,0:T(8,128)(2,1)S(1)}, u32[]{:S(2)}, u32[]{:S(2)}) collective-permute-start(bf16[48,1792]{1,0:T(8,128)(2,1)S(1)} %get-tuple-element.108), channel_id=1, source_target_pairs={{0,2},{2,4},{4,6},{6,8},{8,10},{10,12},{12,14},{14,0},{1,3},{3,5},... | collective-permute-start | bytes 516104 | tf_op jit(solution)/shard_map/ppermute | solution.py:160
  192.7 8.6 %collective-permute-start.25 = (bf16[48,1792]{1,0:T(8,128)(2,1)S(1)}, bf16[48,1792]{1,0:T(8,128)(2,1)S(1)}, u32[]{:S(2)}, u32[]{:S(2)}) collective-permute-start(bf16[48,1792]{1,0:T(8,128)(2,1)S(1)} %get-tuple-element.112), channel_id=1, source_target_pairs={{0,2},{2,4},{4,6},{6,8},{8,10},{10,12},{12,14},{14,0},{1,3},{3,5},... | collective-permute-start | bytes 516104 | tf_op jit(solution)/shard_map/ppermute | solution.py:160
  205.7 8.6 %collective-permute-start.27 = (bf16[48,1792]{1,0:T(8,128)(2,1)S(1)}, bf16[48,1792]{1,0:T(8,128)(2,1)S(1)}, u32[]{:S(2)}, u32[]{:S(2)}) collective-permute-start(bf16[48,1792]{1,0:T(8,128)(2,1)S(1)} %get-tuple-element.116), channel_id=1, source_target_pairs={{0,2},{2,4},{4,6},{6,8},{8,10},{10,12},{12,14},{14,0},{1,3},{3,5},... | collective-permute-start | bytes 516104 | tf_op jit(solution)/shard_map/ppermute | solution.py:160
  218.7 8.6 %collective-permute-start.29 = (bf16[48,1792]{1,0:T(8,128)(2,1)S(1)}, bf16[48,1792]{1,0:T(8,128)(2,1)S(1)}, u32[]{:S(2)}, u32[]{:S(2)}) collective-permute-start(bf16[48,1792]{1,0:T(8,128)(2,1)S(1)} %get-tuple-element.120), channel_id=1, source_target_pairs={{0,2},{2,4},{4,6},{6,8},{8,10},{10,12},{12,14},{14,0},{1,3},{3,5},... | collective-permute-start | bytes 516104 | tf_op jit(solution)/shard_map/ppermute | solution.py:160
  227.3 1.8 collective-permute-start.30
  232.1 8.6 %collective-permute-start.31 = (bf16[48,1792]{1,0:T(8,128)(2,1)S(1)}, bf16[48,1792]{1,0:T(8,128)(2,1)S(1)}, u32[]{:S(2)}, u32[]{:S(2)}) collective-permute-start(bf16[48,1792]{1,0:T(8,128)(2,1)S(1)} %get-tuple-element.124), channel_id=1, source_target_pairs={{0,2},{2,4},{4,6},{6,8},{8,10},{10,12},{12,14},{14,0},{1,3},{3,5},... | collective-permute-start | bytes 516104 | tf_op jit(solution)/shard_map/ppermute | solution.py:160
  245.8 8.8 %collective-permute-start.35 = (bf16[48,1792]{1,0:T(8,128)(2,1)}, bf16[48,1792]{1,0:T(8,128)(2,1)}, u32[]{:S(2)}, u32[]{:S(2)}) collective-permute-start(bf16[48,1792]{1,0:T(8,128)(2,1)} %get-tuple-element.134), channel_id=1, source_target_pairs={{0,2},{2,4},{4,6},{6,8},{8,10},{10,12},{12,14},{14,0},{1,3},{3,5},... | collective-permute-start | bytes 516104 | tf_op jit(solution)/shard_map/ppermute | solution.py:160
  252.8 1.9 collective-permute-start.33
  254.7 5.8 %collective-permute-start.36 = (bf16[48,1792]{1,0:T(8,128)(2,1)}, bf16[48,1792]{1,0:T(8,128)(2,1)S(1)}, u32[]{:S(2)}, u32[]{:S(2)}) collective-permute-start(bf16[48,1792]{1,0:T(8,128)(2,1)} %collective-permute-done.35.own), channel_id=1, source_target_pairs={{0,1},{1,0},{2,3},{3,2},{4,5},{5,4},{6,7},{7,6},{8,9},{9,8},{10,11... | collective-permute-start | bytes 516104 | tf_op jit(solution)/shard_map/ppermute | solution.py:156
  256.6 15.2 %collective-permute-start.34 = (bf16[48,1792]{1,0:T(8,128)(2,1)S(1)}, bf16[48,1792]{1,0:T(8,128)(2,1)S(1)}, u32[]{:S(2)}, u32[]{:S(2)}) collective-permute-start(bf16[48,1792]{1,0:T(8,128)(2,1)S(1)} %get-tuple-element.198), channel_id=1, source_target_pairs={{0,14},{2,0},{4,2},{6,4},{8,6},{10,8},{12,10},{14,12},{1,15},{3,1}... | collective-permute-start | bytes 516104 | tf_op jit(solution)/shard_map/ppermute | solution.py:160
  271.5 8.5 %collective-permute-start.39 = (bf16[48,1792]{1,0:T(8,128)(2,1)S(1)}, bf16[48,1792]{1,0:T(8,128)(2,1)S(1)}, u32[]{:S(2)}, u32[]{:S(2)}) collective-permute-start(bf16[48,1792]{1,0:T(8,128)(2,1)S(1)} %get-tuple-element.142), channel_id=1, source_target_pairs={{0,2},{2,4},{4,6},{6,8},{8,10},{10,12},{12,14},{14,0},{1,3},{3,5},... | collective-permute-start | bytes 516104 | tf_op jit(solution)/shard_map/ppermute | solution.py:160
  276.4 3.6 collective-permute-start.37
  280.0 2.8 collective-permute-start.40
  280.7 6.8 %collective-permute-start.38 = (bf16[48,1792]{1,0:T(8,128)(2,1)S(1)}, bf16[48,1792]{1,0:T(8,128)(2,1)S(1)}, u32[]{:S(2)}, u32[]{:S(2)}) collective-permute-start(bf16[48,1792]{1,0:T(8,128)(2,1)S(1)} %get-tuple-element.196), channel_id=1, source_target_pairs={{0,14},{2,0},{4,2},{6,4},{8,6},{10,8},{12,10},{14,12},{1,15},{3,1}... | collective-permute-start | bytes 516104 | tf_op jit(solution)/shard_map/ppermute | solution.py:160
  294.4 7.9 %collective-permute-start.42 = (bf16[48,1792]{1,0:T(8,128)(2,1)S(1)}, bf16[48,1792]{1,0:T(8,128)(2,1)S(1)}, u32[]{:S(2)}, u32[]{:S(2)}) collective-permute-start(bf16[48,1792]{1,0:T(8,128)(2,1)S(1)} %get-tuple-element.194), channel_id=1, source_target_pairs={{0,14},{2,0},{4,2},{6,4},{8,6},{10,8},{12,10},{14,12},{1,15},{3,1}... | collective-permute-start | bytes 516104 | tf_op jit(solution)/shard_map/ppermute | solution.py:160
  309.2 8.5 %collective-permute-start.44 = (bf16[48,1792]{1,0:T(8,128)(2,1)S(1)}, bf16[48,1792]{1,0:T(8,128)(2,1)S(1)}, u32[]{:S(2)}, u32[]{:S(2)}) collective-permute-start(bf16[48,1792]{1,0:T(8,128)(2,1)S(1)} %get-tuple-element.192), channel_id=1, source_target_pairs={{0,14},{2,0},{4,2},{6,4},{8,6},{10,8},{12,10},{14,12},{1,15},{3,1}... | collective-permute-start | bytes 516104 | tf_op jit(solution)/shard_map/ppermute | solution.py:160
  329.3 8.8 %collective-permute-start.46 = (bf16[48,1792]{1,0:T(8,128)(2,1)}, bf16[48,1792]{1,0:T(8,128)(2,1)S(1)}, u32[]{:S(2)}, u32[]{:S(2)}) collective-permute-start(bf16[48,1792]{1,0:T(8,128)(2,1)} %get-tuple-element.190), channel_id=1, source_target_pairs={{0,14},{2,0},{4,2},{6,4},{8,6},{10,8},{12,10},{14,12},{1,15},{3,1}... | collective-permute-start | bytes 516104 | tf_op jit(solution)/shard_map/ppermute | solution.py:160
  352.5 1.7 collective-permute-start.47
  354.3 9.3 %collective-permute-start.48 = (bf16[48,1792]{1,0:T(8,128)(2,1)S(1)}, bf16[48,1792]{1,0:T(8,128)(2,1)S(1)}, u32[]{:S(2)}, u32[]{:S(2)}) collective-permute-start(bf16[48,1792]{1,0:T(8,128)(2,1)S(1)} %get-tuple-element.188), channel_id=1, source_target_pairs={{0,14},{2,0},{4,2},{6,4},{8,6},{10,8},{12,10},{14,12},{1,15},{3,1}... | collective-permute-start | bytes 516104 | tf_op jit(solution)/shard_map/ppermute | solution.py:160
  369.8 8.6 %collective-permute-start.50 = (bf16[48,1792]{1,0:T(8,128)(2,1)S(1)}, bf16[48,1792]{1,0:T(8,128)(2,1)S(1)}, u32[]{:S(2)}, u32[]{:S(2)}) collective-permute-start(bf16[48,1792]{1,0:T(8,128)(2,1)S(1)} %get-tuple-element.186), channel_id=1, source_target_pairs={{0,14},{2,0},{4,2},{6,4},{8,6},{10,8},{12,10},{14,12},{1,15},{3,1}... | collective-permute-start | bytes 516104 | tf_op jit(solution)/shard_map/ppermute | solution.py:160
  384.6 8.6 %collective-permute-start.52 = (bf16[48,1792]{1,0:T(8,128)(2,1)S(1)}, bf16[48,1792]{1,0:T(8,128)(2,1)S(1)}, u32[]{:S(2)}, u32[]{:S(2)}) collective-permute-start(bf16[48,1792]{1,0:T(8,128)(2,1)S(1)} %get-tuple-element.184), channel_id=1, source_target_pairs={{0,14},{2,0},{4,2},{6,4},{8,6},{10,8},{12,10},{14,12},{1,15},{3,1}... | collective-permute-start | bytes 516104 | tf_op jit(solution)/shard_map/ppermute | solution.py:160
  399.4 8.8 %collective-permute-start.54 = (bf16[48,1792]{1,0:T(8,128)(2,1)S(1)}, bf16[48,1792]{1,0:T(8,128)(2,1)S(1)}, u32[]{:S(2)}, u32[]{:S(2)}) collective-permute-start(bf16[48,1792]{1,0:T(8,128)(2,1)S(1)} %get-tuple-element.182), channel_id=1, source_target_pairs={{0,14},{2,0},{4,2},{6,4},{8,6},{10,8},{12,10},{14,12},{1,15},{3,1}... | collective-permute-start | bytes 516104 | tf_op jit(solution)/shard_map/ppermute | solution.py:160
  424.3 10.5 %collective-permute-start.56 = (bf16[48,1792]{1,0:T(8,128)(2,1)S(1)}, bf16[48,1792]{1,0:T(8,128)(2,1)S(1)}, u32[]{:S(2)}, u32[]{:S(2)}) collective-permute-start(bf16[48,1792]{1,0:T(8,128)(2,1)S(1)} %get-tuple-element.180), channel_id=1, source_target_pairs={{0,14},{2,0},{4,2},{6,4},{8,6},{10,8},{12,10},{14,12},{1,15},{3,1}... | collective-permute-start | bytes 516104 | tf_op jit(solution)/shard_map/ppermute | solution.py:160
  443.3 27.6 %collective-permute-start.58 = (bf16[48,1792]{1,0:T(8,128)(2,1)S(1)}, bf16[48,1792]{1,0:T(8,128)(2,1)S(1)}, u32[]{:S(2)}, u32[]{:S(2)}) collective-permute-start(bf16[48,1792]{1,0:T(8,128)(2,1)S(1)} %get-tuple-element.202), channel_id=1, source_target_pairs={{0,16},{16,32},{32,48},{48,0},{64,80},{80,96},{96,112},{112,64},{1... | collective-permute-start | bytes 516104 | tf_op jit(solution)/shard_map/ppermute | solution.py:170
  445.3 27.5 %collective-permute-start.59 = (bf16[48,1792]{1,0:T(8,128)(2,1)S(1)}, bf16[48,1792]{1,0:T(8,128)(2,1)S(1)}, u32[]{:S(2)}, u32[]{:S(2)}) collective-permute-start(bf16[48,1792]{1,0:T(8,128)(2,1)S(1)} %get-tuple-element.202), channel_id=1, source_target_pairs={{0,48},{16,0},{32,16},{48,32},{64,112},{80,64},{96,80},{112,96},{1... | collective-permute-start | bytes 516104 | tf_op jit(solution)/shard_map/ppermute | solution.py:170
  449.7 25.5 %collective-permute-start.57 = (bf16[48,1792]{1,0:T(8,128)(2,1)S(1)}, bf16[48,1792]{1,0:T(8,128)(2,1)S(1)}, u32[]{:S(2)}, u32[]{:S(2)}) collective-permute-start(bf16[48,1792]{1,0:T(8,128)(2,1)S(1)} %get-tuple-element.173), channel_id=1, source_target_pairs={{0,1},{1,0},{2,3},{3,2},{4,5},{5,4},{6,7},{7,6},{8,9},{9,8},{10,11... | collective-permute-start | bytes 516104 | tf_op jit(solution)/shard_map/ppermute | solution.py:156
  470.9 12.8 %collective-permute-start.60 = (bf16[24,1792]{1,0:T(8,128)(2,1)S(1)}, bf16[24,1792]{1,0:T(8,128)(2,1)S(1)}, u32[]{:S(2)}, u32[]{:S(2)}) collective-permute-start(bf16[24,1792]{1,0:T(8,128)(2,1)S(1)} %slice.136), channel_id=1, source_target_pairs={{0,16},{16,32},{32,48},{48,0},{64,80},{80,96},{96,112},{112,64},{1... | collective-permute-start | bytes 258056 | tf_op jit(solution)/shard_map/ppermute | solution.py:170
  472.8 24.0 %collective-permute-start.61 = (bf16[24,1792]{1,0:T(8,128)(2,1)S(1)}, bf16[24,1792]{1,0:T(8,128)(2,1)S(1)}, u32[]{:S(2)}, u32[]{:S(2)}) collective-permute-start(bf16[24,1792]{1,0:T(8,128)(2,1)S(1)} %slice.137), channel_id=1, source_target_pairs={{0,48},{16,0},{32,16},{48,32},{64,112},{80,64},{96,80},{112,96},{1... | collective-permute-start | bytes 258056 | tf_op jit(solution)/shard_map/ppermute | solution.py:170
  496.8 14.2 %collective-permute-start.62 = (bf16[48,1792]{1,0:T(8,128)(2,1)}, bf16[48,1792]{1,0:T(8,128)(2,1)S(1)}, u32[]{:S(2)}, u32[]{:S(2)}) collective-permute-start(bf16[48,1792]{1,0:T(8,128)(2,1)} %get-tuple-element.177), channel_id=1, source_target_pairs={{0,16},{16,32},{32,48},{48,0},{64,80},{80,96},{96,112},{112,64},{1... | collective-permute-start | bytes 516104 | tf_op jit(solution)/shard_map/ppermute | solution.py:170
  497.6 13.4 %collective-permute-start.63 = (bf16[48,1792]{1,0:T(8,128)(2,1)}, bf16[48,1792]{1,0:T(8,128)(2,1)S(1)}, u32[]{:S(2)}, u32[]{:S(2)}) collective-permute-start(bf16[48,1792]{1,0:T(8,128)(2,1)} %get-tuple-element.177), channel_id=1, source_target_pairs={{0,48},{16,0},{32,16},{48,32},{64,112},{80,64},{96,80},{112,96},{1... | collective-permute-start | bytes 516104 | tf_op jit(solution)/shard_map/ppermute | solution.py:170
  501.2 27.8 %collective-permute-start.67 = (bf16[4,48,1792]{2,1,0:T(8,128)(2,1)S(1)}, bf16[4,48,1792]{2,1,0:T(8,128)(2,1)S(1)}, u32[]{:S(2)}, u32[]{:S(2)}) collective-permute-start(bf16[4,48,1792]{2,1,0:T(8,128)(2,1)S(1)} %bitcast_dynamic-update-slice_fusion.45), channel_id=1, source_target_pairs={{0,64},{16,80},{32,96},{48,112},{64,128},{80,144},{96,160},{112,17... | collective-permute-start | bytes 2064392 | tf_op jit(solution)/shard_map/ppermute | solution.py:165
  501.6 27.5 %collective-permute-start.68 = (bf16[4,48,1792]{2,1,0:T(8,128)(2,1)S(1)}, bf16[4,48,1792]{2,1,0:T(8,128)(2,1)}, u32[]{:S(2)}, u32[]{:S(2)}) collective-permute-start(bf16[4,48,1792]{2,1,0:T(8,128)(2,1)S(1)} %bitcast_dynamic-update-slice_fusion.45), channel_id=1, source_target_pairs={{0,192},{16,208},{32,224},{48,240},{64,0},{80,16},{96,32},{112,48}... | collective-permute-start | bytes 2064392 | tf_op jit(solution)/shard_map/ppermute | solution.py:165
  511.0 6.7 %collective-permute-start.64 = (bf16[24,1792]{1,0:T(8,128)(2,1)S(1)}, bf16[24,1792]{1,0:T(8,128)(2,1)S(1)}, u32[]{:S(2)}, u32[]{:S(2)}) collective-permute-start(bf16[24,1792]{1,0:T(8,128)(2,1)S(1)} %slice.138), channel_id=1, source_target_pairs={{0,16},{16,32},{32,48},{48,0},{64,80},{80,96},{96,112},{112,64},{1... | collective-permute-start | bytes 258056 | tf_op jit(solution)/shard_map/ppermute | solution.py:170
  511.1 6.6 %collective-permute-start.65 = (bf16[24,1792]{1,0:T(8,128)(2,1)S(1)}, bf16[24,1792]{1,0:T(8,128)(2,1)S(1)}, u32[]{:S(2)}, u32[]{:S(2)}) collective-permute-start(bf16[24,1792]{1,0:T(8,128)(2,1)S(1)} %slice.139), channel_id=1, source_target_pairs={{0,48},{16,0},{32,16},{48,32},{64,112},{80,64},{96,80},{112,96},{1... | collective-permute-start | bytes 258056 | tf_op jit(solution)/shard_map/ppermute | solution.py:170
  517.7 24.2 %collective-permute-start.71 = (bf16[4,48,1792]{2,1,0:T(8,128)(2,1)S(1)}, bf16[4,48,1792]{2,1,0:T(8,128)(2,1)}, u32[]{:S(2)}, u32[]{:S(2)}) collective-permute-start(bf16[4,48,1792]{2,1,0:T(8,128)(2,1)S(1)} %bitcast_dynamic-update-slice_fusion.43), channel_id=1, source_target_pairs={{0,64},{16,80},{32,96},{48,112},{64,128},{80,144},{96,160},{112,17... | collective-permute-start | bytes 2064392 | tf_op jit(solution)/shard_map/ppermute | solution.py:165
  517.8 26.8 %collective-permute-start.72 = (bf16[4,48,1792]{2,1,0:T(8,128)(2,1)S(1)}, bf16[4,48,1792]{2,1,0:T(8,128)(2,1)}, u32[]{:S(2)}, u32[]{:S(2)}) collective-permute-start(bf16[4,48,1792]{2,1,0:T(8,128)(2,1)S(1)} %bitcast_dynamic-update-slice_fusion.43), channel_id=1, source_target_pairs={{0,192},{16,208},{32,224},{48,240},{64,0},{80,16},{96,32},{112,48}... | collective-permute-start | bytes 2064392 | tf_op jit(solution)/shard_map/ppermute | solution.py:165
  519.8 39.2 %all-to-all-start = ((bf16[16,96,224]{2,1,0:T(8,128)(2,1)}), bf16[16,96,224]{2,1,0:T(8,128)(2,1)S(1)}, u32[]{:S(2)}, u32[]{:S(2)}) async-start(bf16[16,96,224]{2,1,0:T(8,128)(2,1)} %bitcast.37), calls=%async_computation | async-start | bytes 1572864 | tf_op jit(solution)/shard_map/all_to_all | solution.py:222
  529.0 22.9 %collective-permute-start.69 = (bf16[2,48,1792]{2,1,0:T(8,128)(2,1)S(1)}, bf16[2,48,1792]{2,1,0:T(8,128)(2,1)S(1)}, u32[]{:S(2)}, u32[]{:S(2)}) collective-permute-start(bf16[2,48,1792]{2,1,0:T(8,128)(2,1)S(1)} %slice.140), channel_id=1, source_target_pairs={{0,64},{16,80},{32,96},{48,112},{64,128},{80,144},{96,160},{112,17... | collective-permute-start | bytes 1032200 | tf_op jit(solution)/shard_map/ppermute | solution.py:165
  530.2 23.0 %collective-permute-start.70 = (bf16[2,48,1792]{2,1,0:T(8,128)(2,1)S(1)}, bf16[2,48,1792]{2,1,0:T(8,128)(2,1)S(1)}, u32[]{:S(2)}, u32[]{:S(2)}) collective-permute-start(bf16[2,48,1792]{2,1,0:T(8,128)(2,1)S(1)} %slice.141), channel_id=1, source_target_pairs={{0,192},{16,208},{32,224},{48,240},{64,0},{80,16},{96,32},{112,48}... | collective-permute-start | bytes 1032200 | tf_op jit(solution)/shard_map/ppermute | solution.py:165
  542.9 16.3 %collective-permute-start.73 = (bf16[2,48,1792]{2,1,0:T(8,128)(2,1)S(1)}, bf16[2,48,1792]{2,1,0:T(8,128)(2,1)S(1)}, u32[]{:S(2)}, u32[]{:S(2)}) collective-permute-start(bf16[2,48,1792]{2,1,0:T(8,128)(2,1)S(1)} %slice.142), channel_id=1, source_target_pairs={{0,64},{16,80},{32,96},{48,112},{64,128},{80,144},{96,160},{112,17... | collective-permute-start | bytes 1032200 | tf_op jit(solution)/shard_map/ppermute | solution.py:165
  546.3 13.7 %collective-permute-start.74 = (bf16[2,48,1792]{2,1,0:T(8,128)(2,1)}, bf16[2,48,1792]{2,1,0:T(8,128)(2,1)S(1)}, u32[]{:S(2)}, u32[]{:S(2)}) collective-permute-start(bf16[2,48,1792]{2,1,0:T(8,128)(2,1)} %slice.143), channel_id=1, source_target_pairs={{0,192},{16,208},{32,224},{48,240},{64,0},{80,16},{96,32},{112,48}... | collective-permute-start | bytes 1032200 | tf_op jit(solution)/shard_map/ppermute | solution.py:165
  558.9 2.5 collective-permute-start.66
  (69 other events, 382.8 us)
Sparse Core Ops, SparseCore 0:
  11.0 117.9 all-gather.3
  405.9 106.4 all-gather.5
where the time goes:
time: 590 us; the launch traced here: 578 us
  waiting for transfers between devices  260 us (44%)
  starting transfers between devices  109 us (18%)
  local copies, waits for them, and re-layouts  90 us (15%)
  Pallas kernels  86.2 us (15%)
  between operations  15.5 us (3%)
  other arithmetic  9.37 us (2%)
  matrix products  8.11 us (1%)
    ppermute x20, waiting for transfers between devices, to_section(): lax.ppermute(value, 'section', [(s, (s + step) % SECTIONS) for s in range...  102 us
    ppermute x16, waiting for transfers between devices, along_y(): return lax.ppermute(value, 'island', pairs)  66.3 us
    ppermute x16, waiting for transfers between devices, along_z(): return lax.ppermute(value, 'island', pairs)  61.7 us
    pallas_call x11, Pallas kernels, backward_tick(): pl.pallas_call(functools.partial(backward_kernel, tick, first), out_shape...  51.3 us
    unnamed x110, local copies, waits for them, and re-layouts  48 us
    ppermute x20, starting transfers between devices, to_section(): lax.ppermute(value, 'section', [(s, (s + step) % SECTIONS) for s in range...  45.9 us
    ppermute x16, starting transfers between devices, along_z(): return lax.ppermute(value, 'island', pairs)  35.4 us
    pallas_call x11, Pallas kernels, forward_tick(): pl.pallas_call(functools.partial(forward_kernel, tick, first), out_shape=...  34.9 us
  transfers between devices with their start and end apart: 78, of which 58 were waited for; matrix products, arithmetic and copies ran while one was open for 8% of the time, Pallas kernels for 5%

commit v1 on v0

--- a/solution.py
+++ b/solution.py
@@ -178,7 +178,7 @@
     target = at(target, (place + SIDE - 1) % SIDE, below, 0)
     target = at(target, (place + 1) % SIDE, above, 0)
     target = at(target, (place + 2) % SIDE, far_low, 0)
-    return at(target, (place + 2) % SIDE, far_high, half)
+    return at(target, (place + 2) % SIDE, far_high, half), (below, above)
 
 
 def gather_islands(block, target, row_start):
@@ -195,8 +195,9 @@
             buffer, piece, (position, start, row_start) + (0,) * (buffer.ndim - 3)
         )
 
-    column = ring_gather(block, along_z, z_place, jnp.zeros((SIDE, *block.shape), BF16), at_z)
-    return ring_gather(column, along_y, y_place, target, at_y), column
+    start = jnp.zeros((SIDE, *block.shape), BF16)
+    column, first_round = ring_gather(block, along_z, z_place, start, at_z)
+    return ring_gather(column, along_y, y_place, target, at_y)[0], column, first_round
 
 
 def after(value, earlier):
@@ -209,7 +210,7 @@
     start = 0
     for size in ROW_CHUNKS:
         block = rows[start : start + size, SPLIT:]
-        by_rings, _ = gather_islands(block, by_rings, start)
+        by_rings, _, _ = gather_islands(block, by_rings, start)
         start += size
     return by_gather, by_rings.reshape(D, HALF - SPLIT)
 
@@ -262,9 +263,9 @@
     ring_deltas = jnp.broadcast_to(empty, (SIDE, SIDE, MICRO - EARLY, MB, HALF))
     block = deltas[EARLY]
     for micro in range(EARLY, MICRO):
-        ring_deltas, column = gather_islands(block, ring_deltas, micro - EARLY)
+        ring_deltas, column, first_round = gather_islands(block, ring_deltas, micro - EARLY)
         if micro < MICRO - 1:
-            block = after(deltas[micro + 1], column)
+            block = after(deltas[micro + 1], first_round)
     x_part = exchange_x(x_slots, tp_id, column)
 
     x_other = swap_cores(x_part)

time: 590 us -> 591 us (level)
  starting transfers between devices: 109 us -> 116 us
    ppermute x16, starting transfers between devices: 17.2 us -> 24.6 us  [along_y(): return lax.ppermute(value, 'island', pairs)]
where the time goes in v1:
time: 591 us; the launch traced here: 580 us
  waiting for transfers between devices  255 us (43%)
  starting transfers between devices  116 us (20%)
  local copies, waits for them, and re-layouts  90.1 us (15%)
  Pallas kernels  86.2 us (15%)
  between operations  15.5 us (3%)
  other arithmetic  9.37 us (2%)
  matrix products  8.11 us (1%)
    ppermute x20, waiting for transfers between devices, to_section(): lax.ppermute(value, 'section', [(s, (s + step) % SECTIONS) for s in range...  102 us
    ppermute x16, waiting for transfers between devices, along_y(): return lax.ppermute(value, 'island', pairs)  66.2 us
    ppermute x16, waiting for transfers between devices, along_z(): return lax.ppermute(value, 'island', pairs)  57 us
    pallas_call x11, Pallas kernels, backward_tick(): pl.pallas_call(functools.partial(backward_kernel, tick, first), out_shape...  51.3 us
    unnamed x110, local copies, waits for them, and re-layouts  48 us
    ppermute x20, starting transfers between devices, to_section(): lax.ppermute(value, 'section', [(s, (s + step) % SECTIONS) for s in range...  45.9 us
    ppermute x16, starting transfers between devices, along_z(): return lax.ppermute(value, 'island', pairs)  35.2 us
    pallas_call x11, Pallas kernels, forward_tick(): pl.pallas_call(functools.partial(forward_kernel, tick, first), out_shape=...  34.9 us
  transfers between devices with their start and end apart: 78, of which 58 were waited for; matrix products, arithmetic and copies ran while one was open for 8% of the time, Pallas kernels for 5%

profile of v1, /device:TPU:56, one launch (start us, length us, event | category | flops | bytes accessed | tf_op | source)
XLA Modules:
  0.0 580.0 jit_solution(17650344687438687152)
XLA Ops:
  9.6 3.3 collective-permute-start.1
  22.2 3.9 collective-permute-done.1
  26.1 4.2 collective-permute-start.4
  30.3 5.9 %collective-permute-done.9 = bf16[128,768]{1,0:T(8,128)(2,1)S(1)} collective-permute-done((bf16[128,768]{1,0:T(8,128)(2,1)S(1)}, bf16[128,768]{1,0:T(8,128)(2,1)S(1)}, u32[]{:S(2)}, u32[]{:S(2)}) %collective-permute-start.9) | collective-permute-done | bytes 196640 | tf_op jit(solution)/shard_map/ppermute | solution.py:170
  36.7 3.8 collective-permute-start.12
  52.2 10.7 %collective-permute-done.5 = bf16[4,96,768]{2,1,0:T(8,128)(2,1)} collective-permute-done((bf16[4,96,768]{2,1,0:T(8,128)(2,1)S(1)}, bf16[4,96,768]{2,1,0:T(8,128)(2,1)}, u32[]{:S(2)}, u32[]{:S(2)}) %collective-permute-start.5) | collective-permute-done | bytes 589856 | tf_op jit(solution)/shard_map/ppermute | solution.py:165
  69.5 23.0 %collective-permute-done.13 = bf16[4,128,768]{2,1,0:T(8,128)(2,1)S(1)} collective-permute-done((bf16[4,128,768]{2,1,0:T(8,128)(2,1)S(1)}, bf16[4,128,768]{2,1,0:T(8,128)(2,1)S(1)}, u32[]{:S(2)}, u32[]{:S(2)}) %collective-permute-start.13) | collective-permute-done | bytes 786464 | tf_op jit(solution)/shard_map/ppermute | solution.py:165
  95.9 8.7 %collective-permute-done.7 = bf16[2,96,768]{2,1,0:T(8,128)(2,1)S(1)} collective-permute-done((bf16[2,96,768]{2,1,0:T(8,128)(2,1)S(1)}, bf16[2,96,768]{2,1,0:T(8,128)(2,1)S(1)}, u32[]{:S(2)}, u32[]{:S(2)}) %collective-permute-start.7) | collective-permute-done | bytes 294944 | tf_op jit(solution)/shard_map/ppermute | solution.py:165
  106.8 6.5 %collective-permute-done.15 = bf16[2,128,768]{2,1,0:T(8,128)(2,1)S(1)} collective-permute-done((bf16[2,128,768]{2,1,0:T(8,128)(2,1)S(1)}, bf16[2,128,768]{2,1,0:T(8,128)(2,1)S(1)}, u32[]{:S(2)}, u32[]{:S(2)}) %collective-permute-start.15) | collective-permute-done | bytes 393248 | tf_op jit(solution)/shard_map/ppermute | solution.py:165
  118.3 10.7 %all-gather.4.cloned.1.call-done.weights_a = bf16[3584,1024]{1,0:T(8,128)(2,1)} async-done(((bf16[224,1024]{1,0:T(8,128)(2,1)}), bf16[3584,1024]{1,0:T(8,128)(2,1)}) %all-gather.4.cloned.1.call-update) | async-done | bytes 7340048 | tf_op jit(solution)/shard_map/all_gather | solution.py:208
  129.0 3.1 copy-done
  142.5 6.5 %collective-permute-done.17.own = bf16[48,1792]{1,0:T(8,128)(2,1)S(1)} collective-permute-done((bf16[48,1792]{1,0:T(8,128)(2,1)S(1)}, bf16[48,1792]{1,0:T(8,128)(2,1)S(1)}, u32[]{:S(2)}, u32[]{:S(2)}) %collective-permute-start.17) | collective-permute-done | bytes 172064 | tf_op jit(solution)/shard_map/ppermute | solution.py:160
  153.5 8.5 %collective-permute-done.19.own = bf16[48,1792]{1,0:T(8,128)(2,1)S(1)} collective-permute-done((bf16[48,1792]{1,0:T(8,128)(2,1)S(1)}, bf16[48,1792]{1,0:T(8,128)(2,1)S(1)}, u32[]{:S(2)}, u32[]{:S(2)}) %collective-permute-start.19) | collective-permute-done | bytes 172064 | tf_op jit(solution)/shard_map/ppermute | solution.py:160
  166.5 8.5 %collective-permute-done.21.own = bf16[48,1792]{1,0:T(8,128)(2,1)S(1)} collective-permute-done((bf16[48,1792]{1,0:T(8,128)(2,1)S(1)}, bf16[48,1792]{1,0:T(8,128)(2,1)S(1)}, u32[]{:S(2)}, u32[]{:S(2)}) %collective-permute-start.21) | collective-permute-done | bytes 172064 | tf_op jit(solution)/shard_map/ppermute | solution.py:160
  179.7 8.5 %collective-permute-done.23.own = bf16[48,1792]{1,0:T(8,128)(2,1)S(1)} collective-permute-done((bf16[48,1792]{1,0:T(8,128)(2,1)S(1)}, bf16[48,1792]{1,0:T(8,128)(2,1)S(1)}, u32[]{:S(2)}, u32[]{:S(2)}) %collective-permute-start.23) | collective-permute-done | bytes 172064 | tf_op jit(solution)/shard_map/ppermute | solution.py:160
  192.8 8.5 %collective-permute-done.25.own = bf16[48,1792]{1,0:T(8,128)(2,1)S(1)} collective-permute-done((bf16[48,1792]{1,0:T(8,128)(2,1)S(1)}, bf16[48,1792]{1,0:T(8,128)(2,1)S(1)}, u32[]{:S(2)}, u32[]{:S(2)}) %collective-permute-start.25) | collective-permute-done | bytes 172064 | tf_op jit(solution)/shard_map/ppermute | solution.py:160
  205.8 8.5 %collective-permute-done.27.own = bf16[48,1792]{1,0:T(8,128)(2,1)S(1)} collective-permute-done((bf16[48,1792]{1,0:T(8,128)(2,1)S(1)}, bf16[48,1792]{1,0:T(8,128)(2,1)S(1)}, u32[]{:S(2)}, u32[]{:S(2)}) %collective-permute-start.27) | collective-permute-done | bytes 172064 | tf_op jit(solution)/shard_map/ppermute | solution.py:160
  218.8 8.5 %collective-permute-done.29.own = bf16[48,1792]{1,0:T(8,128)(2,1)S(1)} collective-permute-done((bf16[48,1792]{1,0:T(8,128)(2,1)S(1)}, bf16[48,1792]{1,0:T(8,128)(2,1)S(1)}, u32[]{:S(2)}, u32[]{:S(2)}) %collective-permute-start.29) | collective-permute-done | bytes 172064 | tf_op jit(solution)/shard_map/ppermute | solution.py:160
  232.2 8.5 %collective-permute-done.31.own = bf16[48,1792]{1,0:T(8,128)(2,1)S(1)} collective-permute-done((bf16[48,1792]{1,0:T(8,128)(2,1)S(1)}, bf16[48,1792]{1,0:T(8,128)(2,1)S(1)}, u32[]{:S(2)}, u32[]{:S(2)}) %collective-permute-start.31) | collective-permute-done | bytes 172064 | tf_op jit(solution)/shard_map/ppermute | solution.py:160
  242.1 3.7 forward_tick.19
  245.8 5.3 backward_tick.11
  256.6 3.9 collective-permute-start.34
  260.5 3.1 copy-done.2
  268.0 3.5 forward_tick.20
  271.8 4.6 backward_tick.12
  276.5 3.5 collective-permute-done.39.own
  282.8 3.7 forward_tick.21
  287.5 4.6 backward_tick.13
  294.4 3.9 collective-permute-start.42
  298.3 3.9 collective-permute-done.42.grad
  302.3 4.6 backward_tick.14
  309.2 4.6 collective-permute-start.44
  313.8 3.9 collective-permute-done.44.grad
  321.5 4.6 backward_tick.15
  329.3 4.6 collective-permute-start.46
  333.9 4.3 collective-permute-done.46.grad
  338.1 3.1 copy-done.3
  347.9 4.6 backward_tick.16
  354.3 5.0 collective-permute-start.48
  360.0 3.6 collective-permute-done.48.grad
  363.6 4.6 backward_tick.17
  369.8 4.7 collective-permute-start.50
  375.2 3.3 collective-permute-done.50.grad
  378.4 4.6 backward_tick.18
  384.6 4.7 collective-permute-start.52
  390.0 3.3 collective-permute-done.52.grad
  393.2 4.6 backward_tick.19
  399.4 4.8 collective-permute-start.54
  408.2 3.1 copy-done.4
  418.1 4.6 backward_tick.20
  424.3 4.8 collective-permute-start.56
  429.7 5.1 collective-permute-done.56.grad
  437.9 4.6 backward_tick.21
  449.8 20.6 %collective-permute-done.58 = bf16[48,1792]{1,0:T(8,128)(2,1)S(1)} collective-permute-done((bf16[48,1792]{1,0:T(8,128)(2,1)}, bf16[48,1792]{1,0:T(8,128)(2,1)S(1)}, u32[]{:S(2)}, u32[]{:S(2)}) %collective-permute-start.58) | collective-permute-done | bytes 172064 | tf_op jit(solution)/shard_map/ppermute | solution.py:170
  470.4 4.1 collective-permute-start.61
  474.6 4.4 collective-permute-start.66
  482.7 4.1 collective-permute-done.65
  486.9 12.4 %collective-permute-done.66 = bf16[24,1792]{1,0:T(8,128)(2,1)S(1)} collective-permute-done((bf16[24,1792]{1,0:T(8,128)(2,1)S(1)}, bf16[24,1792]{1,0:T(8,128)(2,1)S(1)}, u32[]{:S(2)}, u32[]{:S(2)}) %collective-permute-start.66) | collective-permute-done | bytes 86048 | tf_op jit(solution)/shard_map/ppermute | solution.py:170
  499.3 5.9 %collective-permute-start.67 = (bf16[4,48,1792]{2,1,0:T(8,128)(2,1)S(1)}, bf16[4,48,1792]{2,1,0:T(8,128)(2,1)S(1)}, u32[]{:S(2)}, u32[]{:S(2)}) collective-permute-start(bf16[4,48,1792]{2,1,0:T(8,128)(2,1)S(1)} %bitcast_dynamic-update-slice_fusion.43), channel_id=1, source_target_pairs={{0,64},{16,80},{32,96},{48,112},{64,128},{80,144},{96,160},{112,17... | collective-permute-start | bytes 2064392 | tf_op jit(solution)/shard_map/ppermute | solution.py:165
  519.4 8.4 %all-to-all-start = ((bf16[16,96,224]{2,1,0:T(8,128)(2,1)}), bf16[16,96,224]{2,1,0:T(8,128)(2,1)S(1)}, u32[]{:S(2)}, u32[]{:S(2)}) async-start(bf16[16,96,224]{2,1,0:T(8,128)(2,1)} %bitcast.37), calls=%async_computation | async-start | bytes 1572864 | tf_op jit(solution)/shard_map/all_to_all | solution.py:223
  533.9 4.5 collective-permute-done.71
  539.4 4.2 collective-permute-start.73
  563.1 4.0 fusion.5
  567.1 4.1 fusion.6
  (327 shorter events, 194.6 us)
Async XLA Ops:
  7.2 121.8 %all-gather.4.cloned.1.call-start = ((), (), s32[]{:S(2)}) async-start(), calls=%async_computation.1 | async-start | bytes 7798784 | tf_op jit(solution)/shard_map/all_gather | solution.py:208
  9.6 557.6 %all-gather.6.cloned.1.call-start = ((), (), s32[]{:S(2)}) async-start(), calls=%async_computation.2 | async-start | bytes 5849088 | tf_op jit(solution)/shard_map/all_gather | solution.py:260
  9.6 16.4 %collective-permute-start.1 = (bf16[96,768]{1,0:T(8,128)(2,1)S(1)}, bf16[96,768]{1,0:T(8,128)(2,1)S(1)}, u32[]{:S(2)}, u32[]{:S(2)}) collective-permute-start(bf16[96,768]{1,0:T(8,128)(2,1)S(1)} %slice.125), channel_id=1, source_target_pairs={{0,16},{16,32},{32,48},{48,0},{64,80},{80,96},{96,112},{112,64},{1... | collective-permute-start | bytes 442376 | tf_op jit(solution)/shard_map/ppermute | solution.py:170
  13.0 13.1 %collective-permute-start.2 = (bf16[96,768]{1,0:T(8,128)(2,1)S(1)}, bf16[96,768]{1,0:T(8,128)(2,1)S(1)}, u32[]{:S(2)}, u32[]{:S(2)}) collective-permute-start(bf16[96,768]{1,0:T(8,128)(2,1)S(1)} %slice.125), channel_id=1, source_target_pairs={{0,48},{16,0},{32,16},{48,32},{64,112},{80,64},{96,80},{112,96},{1... | collective-permute-start | bytes 442376 | tf_op jit(solution)/shard_map/ppermute | solution.py:170
  15.2 21.0 %collective-permute-start.9 = (bf16[128,768]{1,0:T(8,128)(2,1)S(1)}, bf16[128,768]{1,0:T(8,128)(2,1)S(1)}, u32[]{:S(2)}, u32[]{:S(2)}) collective-permute-start(bf16[128,768]{1,0:T(8,128)(2,1)S(1)} %slice.130), channel_id=1, source_target_pairs={{0,16},{16,32},{32,48},{48,0},{64,80},{80,96},{96,112},{112,64},{1... | collective-permute-start | bytes 589832 | tf_op jit(solution)/shard_map/ppermute | solution.py:170
  16.7 20.0 %collective-permute-start.10 = (bf16[128,768]{1,0:T(8,128)(2,1)S(1)}, bf16[128,768]{1,0:T(8,128)(2,1)S(1)}, u32[]{:S(2)}, u32[]{:S(2)}) collective-permute-start(bf16[128,768]{1,0:T(8,128)(2,1)S(1)} %slice.130), channel_id=1, source_target_pairs={{0,48},{16,0},{32,16},{48,32},{64,112},{80,64},{96,80},{112,96},{1... | collective-permute-start | bytes 589832 | tf_op jit(solution)/shard_map/ppermute | solution.py:170
  21.9 95.7 %collective-permute-start = (bf16[48,1792]{1,0:T(8,128)(2,1)S(1)}, bf16[48,1792]{1,0:T(8,128)(2,1)S(1)}, u32[]{:S(2)}, u32[]{:S(2)}) collective-permute-start(bf16[48,1792]{1,0:T(8,128)(2,1)S(1)} %get-tuple-element.92.own), channel_id=1, source_target_pairs={{0,1},{1,0},{2,3},{3,2},{4,5},{5,4},{6,7},{7,6},{8,9},{9,8},{10,11... | collective-permute-start | bytes 516104 | tf_op jit(solution)/shard_map/ppermute | solution.py:156
  26.0 15.8 %collective-permute-start.3 = (bf16[48,768]{1,0:T(8,128)(2,1)S(1)}, bf16[48,768]{1,0:T(8,128)(2,1)S(1)}, u32[]{:S(2)}, u32[]{:S(2)}) collective-permute-start(bf16[48,768]{1,0:T(8,128)(2,1)S(1)} %slice.126), channel_id=1, source_target_pairs={{0,16},{16,32},{32,48},{48,0},{64,80},{80,96},{96,112},{112,64},{1... | collective-permute-start | bytes 221192 | tf_op jit(solution)/shard_map/ppermute | solution.py:170
  26.1 18.1 %collective-permute-start.4 = (bf16[48,768]{1,0:T(8,128)(2,1)S(1)}, bf16[48,768]{1,0:T(8,128)(2,1)S(1)}, u32[]{:S(2)}, u32[]{:S(2)}) collective-permute-start(bf16[48,768]{1,0:T(8,128)(2,1)S(1)} %slice.127), channel_id=1, source_target_pairs={{0,48},{16,0},{32,16},{48,32},{64,112},{80,64},{96,80},{112,96},{1... | collective-permute-start | bytes 221192 | tf_op jit(solution)/shard_map/ppermute | solution.py:170
  36.2 10.5 %collective-permute-start.11 = (bf16[64,768]{1,0:T(8,128)(2,1)S(1)}, bf16[64,768]{1,0:T(8,128)(2,1)S(1)}, u32[]{:S(2)}, u32[]{:S(2)}) collective-permute-start(bf16[64,768]{1,0:T(8,128)(2,1)S(1)} %slice.131), channel_id=1, source_target_pairs={{0,16},{16,32},{32,48},{48,0},{64,80},{80,96},{96,112},{112,64},{1... | collective-permute-start | bytes 294920 | tf_op jit(solution)/shard_map/ppermute | solution.py:170
  36.7 12.7 %collective-permute-start.12 = (bf16[64,768]{1,0:T(8,128)(2,1)S(1)}, bf16[64,768]{1,0:T(8,128)(2,1)S(1)}, u32[]{:S(2)}, u32[]{:S(2)}) collective-permute-start(bf16[64,768]{1,0:T(8,128)(2,1)S(1)} %slice.132), channel_id=1, source_target_pairs={{0,48},{16,0},{32,16},{48,32},{64,112},{80,64},{96,80},{112,96},{1... | collective-permute-start | bytes 294920 | tf_op jit(solution)/shard_map/ppermute | solution.py:170
  44.2 18.7 %collective-permute-start.5 = (bf16[4,96,768]{2,1,0:T(8,128)(2,1)S(1)}, bf16[4,96,768]{2,1,0:T(8,128)(2,1)}, u32[]{:S(2)}, u32[]{:S(2)}) collective-permute-start(bf16[4,96,768]{2,1,0:T(8,128)(2,1)S(1)} %bitcast_dynamic-update-slice_fusion.47), channel_id=1, source_target_pairs={{0,64},{16,80},{32,96},{48,112},{64,128},{80,144},{96,160},{112,17... | collective-permute-start | bytes 1769480 | tf_op jit(solution)/shard_map/ppermute | solution.py:165
  44.3 21.7 %collective-permute-start.6 = (bf16[4,96,768]{2,1,0:T(8,128)(2,1)S(1)}, bf16[4,96,768]{2,1,0:T(8,128)(2,1)}, u32[]{:S(2)}, u32[]{:S(2)}) collective-permute-start(bf16[4,96,768]{2,1,0:T(8,128)(2,1)S(1)} %bitcast_dynamic-update-slice_fusion.47), channel_id=1, source_target_pairs={{0,192},{16,208},{32,224},{48,240},{64,0},{80,16},{96,32},{112,48}... | collective-permute-start | bytes 1769480 | tf_op jit(solution)/shard_map/ppermute | solution.py:165
  49.4 43.1 %collective-permute-start.13 = (bf16[4,128,768]{2,1,0:T(8,128)(2,1)S(1)}, bf16[4,128,768]{2,1,0:T(8,128)(2,1)S(1)}, u32[]{:S(2)}, u32[]{:S(2)}) collective-permute-start(bf16[4,128,768]{2,1,0:T(8,128)(2,1)S(1)} %bitcast_dynamic-update-slice_fusion.41), channel_id=1, source_target_pairs={{0,64},{16,80},{32,96},{48,112},{64,128},{80,144},{96,160},{112,17... | collective-permute-start | bytes 2359304 | tf_op jit(solution)/shard_map/ppermute | solution.py:165
  49.5 45.1 %collective-permute-start.14 = (bf16[4,128,768]{2,1,0:T(8,128)(2,1)S(1)}, bf16[4,128,768]{2,1,0:T(8,128)(2,1)S(1)}, u32[]{:S(2)}, u32[]{:S(2)}) collective-permute-start(bf16[4,128,768]{2,1,0:T(8,128)(2,1)S(1)} %bitcast_dynamic-update-slice_fusion.41), channel_id=1, source_target_pairs={{0,192},{16,208},{32,224},{48,240},{64,0},{80,16},{96,32},{112,48}... | collective-permute-start | bytes 2359304 | tf_op jit(solution)/shard_map/ppermute | solution.py:165
  63.8 40.8 %collective-permute-start.7 = (bf16[2,96,768]{2,1,0:T(8,128)(2,1)S(1)}, bf16[2,96,768]{2,1,0:T(8,128)(2,1)S(1)}, u32[]{:S(2)}, u32[]{:S(2)}) collective-permute-start(bf16[2,96,768]{2,1,0:T(8,128)(2,1)S(1)} %slice.128), channel_id=1, source_target_pairs={{0,64},{16,80},{32,96},{48,112},{64,128},{80,144},{96,160},{112,17... | collective-permute-start | bytes 884744 | tf_op jit(solution)/shard_map/ppermute | solution.py:165
  67.0 39.6 %collective-permute-start.8 = (bf16[2,96,768]{2,1,0:T(8,128)(2,1)S(1)}, bf16[2,96,768]{2,1,0:T(8,128)(2,1)S(1)}, u32[]{:S(2)}, u32[]{:S(2)}) collective-permute-start(bf16[2,96,768]{2,1,0:T(8,128)(2,1)S(1)} %slice.129), channel_id=1, source_target_pairs={{0,192},{16,208},{32,224},{48,240},{64,0},{80,16},{96,32},{112,48}... | collective-permute-start | bytes 884744 | tf_op jit(solution)/shard_map/ppermute | solution.py:165
  92.5 20.8 %collective-permute-start.15 = (bf16[2,128,768]{2,1,0:T(8,128)(2,1)S(1)}, bf16[2,128,768]{2,1,0:T(8,128)(2,1)S(1)}, u32[]{:S(2)}, u32[]{:S(2)}) collective-permute-start(bf16[2,128,768]{2,1,0:T(8,128)(2,1)S(1)} %slice.133), channel_id=1, source_target_pairs={{0,64},{16,80},{32,96},{48,112},{64,128},{80,144},{96,160},{112,17... | collective-permute-start | bytes 1179656 | tf_op jit(solution)/shard_map/ppermute | solution.py:165
  94.7 20.5 %collective-permute-start.16 = (bf16[2,128,768]{2,1,0:T(8,128)(2,1)S(1)}, bf16[2,128,768]{2,1,0:T(8,128)(2,1)S(1)}, u32[]{:S(2)}, u32[]{:S(2)}) collective-permute-start(bf16[2,128,768]{2,1,0:T(8,128)(2,1)S(1)} %slice.134), channel_id=1, source_target_pairs={{0,192},{16,208},{32,224},{48,240},{64,0},{80,16},{96,32},{112,48}... | collective-permute-start | bytes 1179656 | tf_op jit(solution)/shard_map/ppermute | solution.py:165
  140.4 8.5 %collective-permute-start.17 = (bf16[48,1792]{1,0:T(8,128)(2,1)S(1)}, bf16[48,1792]{1,0:T(8,128)(2,1)S(1)}, u32[]{:S(2)}, u32[]{:S(2)}) collective-permute-start(bf16[48,1792]{1,0:T(8,128)(2,1)S(1)} %get-tuple-element.94), channel_id=1, source_target_pairs={{0,2},{2,4},{4,6},{6,8},{8,10},{10,12},{12,14},{14,0},{1,3},{3,5},... | collective-permute-start | bytes 516104 | tf_op jit(solution)/shard_map/ppermute | solution.py:160
  153.4 8.6 %collective-permute-start.19 = (bf16[48,1792]{1,0:T(8,128)(2,1)S(1)}, bf16[48,1792]{1,0:T(8,128)(2,1)S(1)}, u32[]{:S(2)}, u32[]{:S(2)}) collective-permute-start(bf16[48,1792]{1,0:T(8,128)(2,1)S(1)} %get-tuple-element.99), channel_id=1, source_target_pairs={{0,2},{2,4},{4,6},{6,8},{8,10},{10,12},{12,14},{14,0},{1,3},{3,5},... | collective-permute-start | bytes 516104 | tf_op jit(solution)/shard_map/ppermute | solution.py:160
  166.4 8.6 %collective-permute-start.21 = (bf16[48,1792]{1,0:T(8,128)(2,1)S(1)}, bf16[48,1792]{1,0:T(8,128)(2,1)S(1)}, u32[]{:S(2)}, u32[]{:S(2)}) collective-permute-start(bf16[48,1792]{1,0:T(8,128)(2,1)S(1)} %get-tuple-element.104), channel_id=1, source_target_pairs={{0,2},{2,4},{4,6},{6,8},{8,10},{10,12},{12,14},{14,0},{1,3},{3,5},... | collective-permute-start | bytes 516104 | tf_op jit(solution)/shard_map/ppermute | solution.py:160
  179.6 8.6 %collective-permute-start.23 = (bf16[48,1792]{1,0:T(8,128)(2,1)S(1)}, bf16[48,1792]{1,0:T(8,128)(2,1)S(1)}, u32[]{:S(2)}, u32[]{:S(2)}) collective-permute-start(bf16[48,1792]{1,0:T(8,128)(2,1)S(1)} %get-tuple-element.108), channel_id=1, source_target_pairs={{0,2},{2,4},{4,6},{6,8},{8,10},{10,12},{12,14},{14,0},{1,3},{3,5},... | collective-permute-start | bytes 516104 | tf_op jit(solution)/shard_map/ppermute | solution.py:160
  192.7 8.6 %collective-permute-start.25 = (bf16[48,1792]{1,0:T(8,128)(2,1)S(1)}, bf16[48,1792]{1,0:T(8,128)(2,1)S(1)}, u32[]{:S(2)}, u32[]{:S(2)}) collective-permute-start(bf16[48,1792]{1,0:T(8,128)(2,1)S(1)} %get-tuple-element.112), channel_id=1, source_target_pairs={{0,2},{2,4},{4,6},{6,8},{8,10},{10,12},{12,14},{14,0},{1,3},{3,5},... | collective-permute-start | bytes 516104 | tf_op jit(solution)/shard_map/ppermute | solution.py:160
  205.7 8.6 %collective-permute-start.27 = (bf16[48,1792]{1,0:T(8,128)(2,1)S(1)}, bf16[48,1792]{1,0:T(8,128)(2,1)S(1)}, u32[]{:S(2)}, u32[]{:S(2)}) collective-permute-start(bf16[48,1792]{1,0:T(8,128)(2,1)S(1)} %get-tuple-element.116), channel_id=1, source_target_pairs={{0,2},{2,4},{4,6},{6,8},{8,10},{10,12},{12,14},{14,0},{1,3},{3,5},... | collective-permute-start | bytes 516104 | tf_op jit(solution)/shard_map/ppermute | solution.py:160
  218.7 8.6 %collective-permute-start.29 = (bf16[48,1792]{1,0:T(8,128)(2,1)S(1)}, bf16[48,1792]{1,0:T(8,128)(2,1)S(1)}, u32[]{:S(2)}, u32[]{:S(2)}) collective-permute-start(bf16[48,1792]{1,0:T(8,128)(2,1)S(1)} %get-tuple-element.120), channel_id=1, source_target_pairs={{0,2},{2,4},{4,6},{6,8},{8,10},{10,12},{12,14},{14,0},{1,3},{3,5},... | collective-permute-start | bytes 516104 | tf_op jit(solution)/shard_map/ppermute | solution.py:160
  227.3 1.8 collective-permute-start.30
  232.1 8.6 %collective-permute-start.31 = (bf16[48,1792]{1,0:T(8,128)(2,1)S(1)}, bf16[48,1792]{1,0:T(8,128)(2,1)S(1)}, u32[]{:S(2)}, u32[]{:S(2)}) collective-permute-start(bf16[48,1792]{1,0:T(8,128)(2,1)S(1)} %get-tuple-element.124), channel_id=1, source_target_pairs={{0,2},{2,4},{4,6},{6,8},{8,10},{10,12},{12,14},{14,0},{1,3},{3,5},... | collective-permute-start | bytes 516104 | tf_op jit(solution)/shard_map/ppermute | solution.py:160
  245.8 8.8 %collective-permute-start.35 = (bf16[48,1792]{1,0:T(8,128)(2,1)}, bf16[48,1792]{1,0:T(8,128)(2,1)}, u32[]{:S(2)}, u32[]{:S(2)}) collective-permute-start(bf16[48,1792]{1,0:T(8,128)(2,1)} %get-tuple-element.134), channel_id=1, source_target_pairs={{0,2},{2,4},{4,6},{6,8},{8,10},{10,12},{12,14},{14,0},{1,3},{3,5},... | collective-permute-start | bytes 516104 | tf_op jit(solution)/shard_map/ppermute | solution.py:160
  252.8 1.9 collective-permute-start.33
  254.7 5.8 %collective-permute-start.36 = (bf16[48,1792]{1,0:T(8,128)(2,1)}, bf16[48,1792]{1,0:T(8,128)(2,1)S(1)}, u32[]{:S(2)}, u32[]{:S(2)}) collective-permute-start(bf16[48,1792]{1,0:T(8,128)(2,1)} %collective-permute-done.35.own), channel_id=1, source_target_pairs={{0,1},{1,0},{2,3},{3,2},{4,5},{5,4},{6,7},{7,6},{8,9},{9,8},{10,11... | collective-permute-start | bytes 516104 | tf_op jit(solution)/shard_map/ppermute | solution.py:156
  256.6 15.2 %collective-permute-start.34 = (bf16[48,1792]{1,0:T(8,128)(2,1)S(1)}, bf16[48,1792]{1,0:T(8,128)(2,1)S(1)}, u32[]{:S(2)}, u32[]{:S(2)}) collective-permute-start(bf16[48,1792]{1,0:T(8,128)(2,1)S(1)} %get-tuple-element.198), channel_id=1, source_target_pairs={{0,14},{2,0},{4,2},{6,4},{8,6},{10,8},{12,10},{14,12},{1,15},{3,1}... | collective-permute-start | bytes 516104 | tf_op jit(solution)/shard_map/ppermute | solution.py:160
  271.5 8.5 %collective-permute-start.39 = (bf16[48,1792]{1,0:T(8,128)(2,1)S(1)}, bf16[48,1792]{1,0:T(8,128)(2,1)S(1)}, u32[]{:S(2)}, u32[]{:S(2)}) collective-permute-start(bf16[48,1792]{1,0:T(8,128)(2,1)S(1)} %get-tuple-element.142), channel_id=1, source_target_pairs={{0,2},{2,4},{4,6},{6,8},{8,10},{10,12},{12,14},{14,0},{1,3},{3,5},... | collective-permute-start | bytes 516104 | tf_op jit(solution)/shard_map/ppermute | solution.py:160
  276.4 3.6 collective-permute-start.37
  280.0 2.8 collective-permute-start.40
  280.7 6.8 %collective-permute-start.38 = (bf16[48,1792]{1,0:T(8,128)(2,1)S(1)}, bf16[48,1792]{1,0:T(8,128)(2,1)S(1)}, u32[]{:S(2)}, u32[]{:S(2)}) collective-permute-start(bf16[48,1792]{1,0:T(8,128)(2,1)S(1)} %get-tuple-element.196), channel_id=1, source_target_pairs={{0,14},{2,0},{4,2},{6,4},{8,6},{10,8},{12,10},{14,12},{1,15},{3,1}... | collective-permute-start | bytes 516104 | tf_op jit(solution)/shard_map/ppermute | solution.py:160
  294.4 7.9 %collective-permute-start.42 = (bf16[48,1792]{1,0:T(8,128)(2,1)S(1)}, bf16[48,1792]{1,0:T(8,128)(2,1)S(1)}, u32[]{:S(2)}, u32[]{:S(2)}) collective-permute-start(bf16[48,1792]{1,0:T(8,128)(2,1)S(1)} %get-tuple-element.194), channel_id=1, source_target_pairs={{0,14},{2,0},{4,2},{6,4},{8,6},{10,8},{12,10},{14,12},{1,15},{3,1}... | collective-permute-start | bytes 516104 | tf_op jit(solution)/shard_map/ppermute | solution.py:160
  309.2 8.5 %collective-permute-start.44 = (bf16[48,1792]{1,0:T(8,128)(2,1)S(1)}, bf16[48,1792]{1,0:T(8,128)(2,1)S(1)}, u32[]{:S(2)}, u32[]{:S(2)}) collective-permute-start(bf16[48,1792]{1,0:T(8,128)(2,1)S(1)} %get-tuple-element.192), channel_id=1, source_target_pairs={{0,14},{2,0},{4,2},{6,4},{8,6},{10,8},{12,10},{14,12},{1,15},{3,1}... | collective-permute-start | bytes 516104 | tf_op jit(solution)/shard_map/ppermute | solution.py:160
  329.3 8.8 %collective-permute-start.46 = (bf16[48,1792]{1,0:T(8,128)(2,1)}, bf16[48,1792]{1,0:T(8,128)(2,1)S(1)}, u32[]{:S(2)}, u32[]{:S(2)}) collective-permute-start(bf16[48,1792]{1,0:T(8,128)(2,1)} %get-tuple-element.190), channel_id=1, source_target_pairs={{0,14},{2,0},{4,2},{6,4},{8,6},{10,8},{12,10},{14,12},{1,15},{3,1}... | collective-permute-start | bytes 516104 | tf_op jit(solution)/shard_map/ppermute | solution.py:160
  352.5 1.7 collective-permute-start.47
  354.3 9.3 %collective-permute-start.48 = (bf16[48,1792]{1,0:T(8,128)(2,1)S(1)}, bf16[48,1792]{1,0:T(8,128)(2,1)S(1)}, u32[]{:S(2)}, u32[]{:S(2)}) collective-permute-start(bf16[48,1792]{1,0:T(8,128)(2,1)S(1)} %get-tuple-element.188), channel_id=1, source_target_pairs={{0,14},{2,0},{4,2},{6,4},{8,6},{10,8},{12,10},{14,12},{1,15},{3,1}... | collective-permute-start | bytes 516104 | tf_op jit(solution)/shard_map/ppermute | solution.py:160
  369.8 8.6 %collective-permute-start.50 = (bf16[48,1792]{1,0:T(8,128)(2,1)S(1)}, bf16[48,1792]{1,0:T(8,128)(2,1)S(1)}, u32[]{:S(2)}, u32[]{:S(2)}) collective-permute-start(bf16[48,1792]{1,0:T(8,128)(2,1)S(1)} %get-tuple-element.186), channel_id=1, source_target_pairs={{0,14},{2,0},{4,2},{6,4},{8,6},{10,8},{12,10},{14,12},{1,15},{3,1}... | collective-permute-start | bytes 516104 | tf_op jit(solution)/shard_map/ppermute | solution.py:160
  384.6 8.6 %collective-permute-start.52 = (bf16[48,1792]{1,0:T(8,128)(2,1)S(1)}, bf16[48,1792]{1,0:T(8,128)(2,1)S(1)}, u32[]{:S(2)}, u32[]{:S(2)}) collective-permute-start(bf16[48,1792]{1,0:T(8,128)(2,1)S(1)} %get-tuple-element.184), channel_id=1, source_target_pairs={{0,14},{2,0},{4,2},{6,4},{8,6},{10,8},{12,10},{14,12},{1,15},{3,1}... | collective-permute-start | bytes 516104 | tf_op jit(solution)/shard_map/ppermute | solution.py:160
  399.4 8.8 %collective-permute-start.54 = (bf16[48,1792]{1,0:T(8,128)(2,1)S(1)}, bf16[48,1792]{1,0:T(8,128)(2,1)S(1)}, u32[]{:S(2)}, u32[]{:S(2)}) collective-permute-start(bf16[48,1792]{1,0:T(8,128)(2,1)S(1)} %get-tuple-element.182), channel_id=1, source_target_pairs={{0,14},{2,0},{4,2},{6,4},{8,6},{10,8},{12,10},{14,12},{1,15},{3,1}... | collective-permute-start | bytes 516104 | tf_op jit(solution)/shard_map/ppermute | solution.py:160
  424.3 10.5 %collective-permute-start.56 = (bf16[48,1792]{1,0:T(8,128)(2,1)S(1)}, bf16[48,1792]{1,0:T(8,128)(2,1)S(1)}, u32[]{:S(2)}, u32[]{:S(2)}) collective-permute-start(bf16[48,1792]{1,0:T(8,128)(2,1)S(1)} %get-tuple-element.180), channel_id=1, source_target_pairs={{0,14},{2,0},{4,2},{6,4},{8,6},{10,8},{12,10},{14,12},{1,15},{3,1}... | collective-permute-start | bytes 516104 | tf_op jit(solution)/shard_map/ppermute | solution.py:160
  443.3 27.1 %collective-permute-start.58 = (bf16[48,1792]{1,0:T(8,128)(2,1)}, bf16[48,1792]{1,0:T(8,128)(2,1)S(1)}, u32[]{:S(2)}, u32[]{:S(2)}) collective-permute-start(bf16[48,1792]{1,0:T(8,128)(2,1)} %get-tuple-element.203), channel_id=1, source_target_pairs={{0,16},{16,32},{32,48},{48,0},{64,80},{80,96},{96,112},{112,64},{1... | collective-permute-start | bytes 516104 | tf_op jit(solution)/shard_map/ppermute | solution.py:170
  445.3 25.0 %collective-permute-start.59 = (bf16[48,1792]{1,0:T(8,128)(2,1)}, bf16[48,1792]{1,0:T(8,128)(2,1)S(1)}, u32[]{:S(2)}, u32[]{:S(2)}) collective-permute-start(bf16[48,1792]{1,0:T(8,128)(2,1)} %get-tuple-element.203), channel_id=1, source_target_pairs={{0,48},{16,0},{32,16},{48,32},{64,112},{80,64},{96,80},{112,96},{1... | collective-permute-start | bytes 516104 | tf_op jit(solution)/shard_map/ppermute | solution.py:170
  449.8 30.2 %collective-permute-start.57 = (bf16[48,1792]{1,0:T(8,128)(2,1)S(1)}, bf16[48,1792]{1,0:T(8,128)(2,1)S(1)}, u32[]{:S(2)}, u32[]{:S(2)}) collective-permute-start(bf16[48,1792]{1,0:T(8,128)(2,1)S(1)} %get-tuple-element.173), channel_id=1, source_target_pairs={{0,1},{1,0},{2,3},{3,2},{4,5},{5,4},{6,7},{7,6},{8,9},{9,8},{10,11... | collective-permute-start | bytes 516104 | tf_op jit(solution)/shard_map/ppermute | solution.py:156
  470.4 38.6 %collective-permute-start.60 = (bf16[48,1792]{1,0:T(8,128)(2,1)}, bf16[48,1792]{1,0:T(8,128)(2,1)S(1)}, u32[]{:S(2)}, u32[]{:S(2)}) collective-permute-start(bf16[48,1792]{1,0:T(8,128)(2,1)} %get-tuple-element.177), channel_id=1, source_target_pairs={{0,16},{16,32},{32,48},{48,0},{64,80},{80,96},{96,112},{112,64},{1... | collective-permute-start | bytes 516104 | tf_op jit(solution)/shard_map/ppermute | solution.py:170
  470.4 40.2 %collective-permute-start.61 = (bf16[48,1792]{1,0:T(8,128)(2,1)}, bf16[48,1792]{1,0:T(8,128)(2,1)S(1)}, u32[]{:S(2)}, u32[]{:S(2)}) collective-permute-start(bf16[48,1792]{1,0:T(8,128)(2,1)} %get-tuple-element.177), channel_id=1, source_target_pairs={{0,48},{16,0},{32,16},{48,32},{64,112},{80,64},{96,80},{112,96},{1... | collective-permute-start | bytes 516104 | tf_op jit(solution)/shard_map/ppermute | solution.py:170
  474.5 12.3 %collective-permute-start.65 = (bf16[24,1792]{1,0:T(8,128)(2,1)S(1)}, bf16[24,1792]{1,0:T(8,128)(2,1)S(1)}, u32[]{:S(2)}, u32[]{:S(2)}) collective-permute-start(bf16[24,1792]{1,0:T(8,128)(2,1)S(1)} %slice.138), channel_id=1, source_target_pairs={{0,16},{16,32},{32,48},{48,0},{64,80},{80,96},{96,112},{112,64},{1... | collective-permute-start | bytes 258056 | tf_op jit(solution)/shard_map/ppermute | solution.py:170
  474.6 24.7 %collective-permute-start.66 = (bf16[24,1792]{1,0:T(8,128)(2,1)S(1)}, bf16[24,1792]{1,0:T(8,128)(2,1)S(1)}, u32[]{:S(2)}, u32[]{:S(2)}) collective-permute-start(bf16[24,1792]{1,0:T(8,128)(2,1)S(1)} %slice.139), channel_id=1, source_target_pairs={{0,48},{16,0},{32,16},{48,32},{64,112},{80,64},{96,80},{112,96},{1... | collective-permute-start | bytes 258056 | tf_op jit(solution)/shard_map/ppermute | solution.py:170
  499.3 28.5 %collective-permute-start.67 = (bf16[4,48,1792]{2,1,0:T(8,128)(2,1)S(1)}, bf16[4,48,1792]{2,1,0:T(8,128)(2,1)S(1)}, u32[]{:S(2)}, u32[]{:S(2)}) collective-permute-start(bf16[4,48,1792]{2,1,0:T(8,128)(2,1)S(1)} %bitcast_dynamic-update-slice_fusion.43), channel_id=1, source_target_pairs={{0,64},{16,80},{32,96},{48,112},{64,128},{80,144},{96,160},{112,17... | collective-permute-start | bytes 2064392 | tf_op jit(solution)/shard_map/ppermute | solution.py:165
  505.2 22.8 %collective-permute-start.68 = (bf16[4,48,1792]{2,1,0:T(8,128)(2,1)S(1)}, bf16[4,48,1792]{2,1,0:T(8,128)(2,1)}, u32[]{:S(2)}, u32[]{:S(2)}) collective-permute-start(bf16[4,48,1792]{2,1,0:T(8,128)(2,1)S(1)} %bitcast_dynamic-update-slice_fusion.43), channel_id=1, source_target_pairs={{0,192},{16,208},{32,224},{48,240},{64,0},{80,16},{96,32},{112,48}... | collective-permute-start | bytes 2064392 | tf_op jit(solution)/shard_map/ppermute | solution.py:165
  509.0 6.7 %collective-permute-start.62 = (bf16[24,1792]{1,0:T(8,128)(2,1)S(1)}, bf16[24,1792]{1,0:T(8,128)(2,1)S(1)}, u32[]{:S(2)}, u32[]{:S(2)}) collective-permute-start(bf16[24,1792]{1,0:T(8,128)(2,1)S(1)} %slice.136), channel_id=1, source_target_pairs={{0,16},{16,32},{32,48},{48,0},{64,80},{80,96},{96,112},{112,64},{1... | collective-permute-start | bytes 258056 | tf_op jit(solution)/shard_map/ppermute | solution.py:170
  510.6 6.1 %collective-permute-start.63 = (bf16[24,1792]{1,0:T(8,128)(2,1)S(1)}, bf16[24,1792]{1,0:T(8,128)(2,1)S(1)}, u32[]{:S(2)}, u32[]{:S(2)}) collective-permute-start(bf16[24,1792]{1,0:T(8,128)(2,1)S(1)} %slice.137), channel_id=1, source_target_pairs={{0,48},{16,0},{32,16},{48,32},{64,112},{80,64},{96,80},{112,96},{1... | collective-permute-start | bytes 258056 | tf_op jit(solution)/shard_map/ppermute | solution.py:170
  516.7 21.7 %collective-permute-start.71 = (bf16[4,48,1792]{2,1,0:T(8,128)(2,1)S(1)}, bf16[4,48,1792]{2,1,0:T(8,128)(2,1)}, u32[]{:S(2)}, u32[]{:S(2)}) collective-permute-start(bf16[4,48,1792]{2,1,0:T(8,128)(2,1)S(1)} %bitcast_dynamic-update-slice_fusion.45), channel_id=1, source_target_pairs={{0,64},{16,80},{32,96},{48,112},{64,128},{80,144},{96,160},{112,17... | collective-permute-start | bytes 2064392 | tf_op jit(solution)/shard_map/ppermute | solution.py:165
  519.4 27.1 %collective-permute-start.72 = (bf16[4,48,1792]{2,1,0:T(8,128)(2,1)S(1)}, bf16[4,48,1792]{2,1,0:T(8,128)(2,1)}, u32[]{:S(2)}, u32[]{:S(2)}) collective-permute-start(bf16[4,48,1792]{2,1,0:T(8,128)(2,1)S(1)} %bitcast_dynamic-update-slice_fusion.45), channel_id=1, source_target_pairs={{0,192},{16,208},{32,224},{48,240},{64,0},{80,16},{96,32},{112,48}... | collective-permute-start | bytes 2064392 | tf_op jit(solution)/shard_map/ppermute | solution.py:165
  519.4 41.1 %all-to-all-start = ((bf16[16,96,224]{2,1,0:T(8,128)(2,1)}), bf16[16,96,224]{2,1,0:T(8,128)(2,1)S(1)}, u32[]{:S(2)}, u32[]{:S(2)}) async-start(bf16[16,96,224]{2,1,0:T(8,128)(2,1)} %bitcast.37), calls=%async_computation | async-start | bytes 1572864 | tf_op jit(solution)/shard_map/all_to_all | solution.py:223
  527.8 23.3 %collective-permute-start.69 = (bf16[2,48,1792]{2,1,0:T(8,128)(2,1)S(1)}, bf16[2,48,1792]{2,1,0:T(8,128)(2,1)S(1)}, u32[]{:S(2)}, u32[]{:S(2)}) collective-permute-start(bf16[2,48,1792]{2,1,0:T(8,128)(2,1)S(1)} %slice.140), channel_id=1, source_target_pairs={{0,64},{16,80},{32,96},{48,112},{64,128},{80,144},{96,160},{112,17... | collective-permute-start | bytes 1032200 | tf_op jit(solution)/shard_map/ppermute | solution.py:165
  529.0 25.8 %collective-permute-start.70 = (bf16[2,48,1792]{2,1,0:T(8,128)(2,1)S(1)}, bf16[2,48,1792]{2,1,0:T(8,128)(2,1)S(1)}, u32[]{:S(2)}, u32[]{:S(2)}) collective-permute-start(bf16[2,48,1792]{2,1,0:T(8,128)(2,1)S(1)} %slice.141), channel_id=1, source_target_pairs={{0,192},{16,208},{32,224},{48,240},{64,0},{80,16},{96,32},{112,48}... | collective-permute-start | bytes 1032200 | tf_op jit(solution)/shard_map/ppermute | solution.py:165
  539.4 21.3 %collective-permute-start.73 = (bf16[2,48,1792]{2,1,0:T(8,128)(2,1)S(1)}, bf16[2,48,1792]{2,1,0:T(8,128)(2,1)S(1)}, u32[]{:S(2)}, u32[]{:S(2)}) collective-permute-start(bf16[2,48,1792]{2,1,0:T(8,128)(2,1)S(1)} %slice.142), channel_id=1, source_target_pairs={{0,64},{16,80},{32,96},{48,112},{64,128},{80,144},{96,160},{112,17... | collective-permute-start | bytes 1032200 | tf_op jit(solution)/shard_map/ppermute | solution.py:165
  548.2 13.3 %collective-permute-start.74 = (bf16[2,48,1792]{2,1,0:T(8,128)(2,1)}, bf16[2,48,1792]{2,1,0:T(8,128)(2,1)S(1)}, u32[]{:S(2)}, u32[]{:S(2)}) collective-permute-start(bf16[2,48,1792]{2,1,0:T(8,128)(2,1)} %slice.143), channel_id=1, source_target_pairs={{0,192},{16,208},{32,224},{48,240},{64,0},{80,16},{96,32},{112,48}... | collective-permute-start | bytes 1032200 | tf_op jit(solution)/shard_map/ppermute | solution.py:165
  560.5 2.5 collective-permute-start.64
  (69 other events, 382.8 us)
Sparse Core Ops, SparseCore 0:
  11.0 117.9 all-gather.3
  405.9 104.6 all-gather.5
